TPU v7x, 32 devices: a whole 2x2x4 slice. The times are simulated.
32 devices in a mesh: region: 8 (over y, x, core), pos: 4 (over z).
Axes of the slice: x: 2, y: 2, z: 4, core: 2. Of those that a mesh axis runs over, the one named last changes fastest.
Arguments:
- object_tiles: float32 [128, 2, 2, 128, 128], P('region'), may hold values from -4 to 4
- probe: float32 [4, 2, 256, 256], replicated, may hold values from -3 to 3
- fresnel_phase: float32 [256, 256], replicated, may hold values from -3.140625 to 3.140625
- patterns: float32 [8, 4, 2, 256, 256], P('region', 'pos'), may hold values from 0 to 4
- row_offsets: int32 [8, 4, 2], P('region', 'pos'), may hold values from 0 to 1792, as said below
- col_offsets: int32 [8, 4, 2], P('region', 'pos'), may hold values from 0 to 768
- counts: int32 [8, 4], P('region', 'pos'), may hold values from 1 to 2, as said below
Outputs:
- new_object: float32 [128, 2, 2, 128, 128], P('region')
Inputs may be any that keep to these rules, and one draw needn't show every extreme that they name: A device's live positions are its first counts slots; the other slots of its position arrays are ignored. Some device holds 2 live positions. `row_offsets`: every slot of region index r starts at a row from r * 2 * 128 to r * 2 * 128 + 2 * 128 - 1, and never after row 1792.
All inputs are finite; a program needn't handle non-finite values.
Results may differ from a plain program's by a relative error of at most 0.0095.
Values sent between devices are 32-bit elements; how exact they have to be, the bound alone decides.
A program may use at most 128 MiB of HBM per device.

v0:
```python
import math

import jax
import jax.numpy as jnp
from jax import lax
from jax.sharding import PartitionSpec as P

TGX = 8


step_size = 0.05


def shifted(shard, axis, by):
    count = lax.axis_size(axis)
    pairs = [(i, i + by) for i in range(count) if 0 <= i + by < count]
    return lax.ppermute(shard, axis, pairs)


def make_tables(length):
    counter = jnp.arange(length, dtype=jnp.int32)
    product = counter[:, None] * counter[None, :] % length
    angles = product.astype(jnp.float32) * jnp.float32(2.0 * math.pi / length)
    factor = jnp.float32(1.0 / math.sqrt(length))
    return (
        (jnp.cos(angles) * factor).astype(jnp.bfloat16),
        (jnp.sin(angles) * factor).astype(jnp.bfloat16),
    )


def left_product(matrix, field):
    return jnp.einsum("jk,mkl->mjl", matrix, field, preferred_element_type=jnp.float32)


def right_product(field, matrix):
    return jnp.einsum("mjk,kl->mjl", field, matrix, preferred_element_type=jnp.float32)


def transform(field_re, field_im, direction, cos_table, sin_table):
    upper_re = left_product(cos_table, field_re) - direction * left_product(sin_table, field_im)
    upper_im = left_product(cos_table, field_im) + direction * left_product(sin_table, field_re)
    upper_re = upper_re.astype(jnp.bfloat16)
    upper_im = upper_im.astype(jnp.bfloat16)
    result_re = right_product(upper_re, cos_table) - direction * right_product(upper_im, sin_table)
    result_im = right_product(upper_im, cos_table) + direction * right_product(upper_re, sin_table)
    return (result_re, result_im)


def complex_product(left_re, left_im, right_re, right_im):
    return (left_re * right_re - left_im * right_im, left_re * right_im + left_im * right_re)


def conj_product(left_re, left_im, right_re, right_im):
    return (left_re * right_re + left_im * right_im, left_re * right_im - left_im * right_re)


def position_gradient(patch, probe, wave_re, wave_im, measured, cos_table, sin_table):
    slice_count = patch.shape[0]
    field_re = probe[:, 0]
    field_im = probe[:, 1]
    incoming = []
    for layer_index in range(slice_count):
        incoming.append((field_re, field_im))
        exit_re, exit_im = complex_product(
            field_re, field_im, patch[layer_index, 0], patch[layer_index, 1]
        )
        exit_re = exit_re.astype(jnp.bfloat16)
        exit_im = exit_im.astype(jnp.bfloat16)
        if layer_index + 1 < slice_count:
            spec_re, spec_im = transform(exit_re, exit_im, -1.0, cos_table, sin_table)
            spec_re, spec_im = complex_product(wave_re, wave_im, spec_re, spec_im)
            field_re, field_im = transform(
                spec_re.astype(jnp.bfloat16),
                spec_im.astype(jnp.bfloat16),
                1.0,
                cos_table,
                sin_table,
            )
    far_re, far_im = transform(exit_re, exit_im, -1.0, cos_table, sin_table)
    intensity = jnp.sum(far_re * far_re + far_im * far_im, axis=0)
    misfit = intensity - measured
    back_re, back_im = transform(
        (misfit * far_re).astype(jnp.bfloat16),
        (misfit * far_im).astype(jnp.bfloat16),
        1.0,
        cos_table,
        sin_table,
    )
    results = [None] * slice_count
    for layer_index in reversed(range(slice_count)):
        incident_re, incident_im = incoming[layer_index]
        grad_re, grad_im = conj_product(incident_re, incident_im, back_re, back_im)
        results[layer_index] = jnp.stack([jnp.sum(grad_re, axis=0), jnp.sum(grad_im, axis=0)])
        if layer_index > 0:
            prior_re, prior_im = conj_product(
                patch[layer_index, 0], patch[layer_index, 1], back_re, back_im
            )
            spec_re, spec_im = transform(
                prior_re.astype(jnp.bfloat16),
                prior_im.astype(jnp.bfloat16),
                -1.0,
                cos_table,
                sin_table,
            )
            spec_re, spec_im = conj_product(wave_re, wave_im, spec_re, spec_im)
            back_re, back_im = transform(
                spec_re.astype(jnp.bfloat16),
                spec_im.astype(jnp.bfloat16),
                1.0,
                cos_table,
                sin_table,
            )
    return jnp.stack(results)


def tiles_to_band(tiles, band_tiles, tile_side):
    slice_count = tiles.shape[1]
    across = tiles.shape[0] // band_tiles
    shaped = tiles.reshape(band_tiles, across, slice_count, 2, tile_side, tile_side).transpose(
        2, 3, 0, 4, 1, 5
    )
    return shaped.reshape(slice_count, 2, band_tiles * tile_side, across * tile_side)


def per_device(object_tiles, probe, fresnel_phase, patterns, row_offsets, col_offsets, counts):
    slot_count = patterns.shape[2]
    pattern_side = patterns.shape[-1]
    tile_side = object_tiles.shape[-1]
    slice_count = object_tiles.shape[1]
    held_tiles = object_tiles.shape[0]
    band_tiles = held_tiles // TGX
    band_rows = band_tiles * tile_side
    width_pixels = TGX * tile_side
    measured = patterns.reshape(slot_count, pattern_side, pattern_side)
    row_start = row_offsets.reshape(slot_count)
    col_start = col_offsets.reshape(slot_count)
    live_count = counts.reshape(())
    following = shifted(object_tiles, "region", -1)
    canvas = jnp.concatenate(
        [
            tiles_to_band(object_tiles, band_tiles, tile_side),
            tiles_to_band(following, band_tiles, tile_side),
        ],
        axis=2,
    )
    band_first = lax.axis_index("region") * band_rows
    cos_table, sin_table = make_tables(pattern_side)
    wave_re = jnp.cos(fresnel_phase)
    wave_im = jnp.sin(fresnel_phase)
    zero_index = jnp.int32(0)

    def one_position(position, gradient):
        local_row = row_start[position] - band_first
        local_col = col_start[position]
        corner = (zero_index, zero_index, local_row, local_col)
        patch = lax.dynamic_slice(canvas, corner, (slice_count, 2, pattern_side, pattern_side))
        term = position_gradient(
            patch, probe, wave_re, wave_im, measured[position], cos_table, sin_table
        )
        former = lax.dynamic_slice(gradient, corner, (slice_count, 2, pattern_side, pattern_side))
        return lax.dynamic_update_slice(gradient, former + term, corner)

    empty = jnp.zeros((slice_count, 2, 2 * band_rows, width_pixels), jnp.float32)
    gradient = lax.fori_loop(0, live_count, one_position, empty)
    shaped = gradient.reshape(slice_count, 2, 2, band_tiles, tile_side, TGX, tile_side).transpose(
        2, 3, 5, 0, 1, 4, 6
    )
    shaped = shaped.reshape(2, held_tiles * slice_count * 2 * tile_side, tile_side)
    own_rows = shaped[0]
    spill_rows = shaped[1]
    held_rows = object_tiles.reshape(-1, tile_side)
    arrived = shifted(spill_rows, "region", 1)
    combined = lax.psum(own_rows + arrived, "pos")
    return (held_rows - step_size * combined).reshape(object_tiles.shape)


def solution(mesh):
    in_specs = (
        P("region", None, None, None, None),
        P(),
        P(),
        P("region", "pos", None, None, None),
        P("region", "pos", None),
        P("region", "pos", None),
        P("region", "pos"),
    )
    out_specs = P("region", None, None, None, None)
    return jax.shard_map(
        per_device, mesh=mesh, in_specs=in_specs, out_specs=out_specs, check_vma=False
    )
```

profile of v0, /device:TPU:2, one launch (start us, length us, event | category | flops | bytes accessed | tf_op | source)
XLA Modules:
  0.0 488.3 jit_solution(564776054181016329)
XLA Ops:
  6.5 1.9 collective-permute-start
  8.5 1.9 copy.58
  11.3 4.4 copy.113
  15.7 4.9 %reshape.50 = f32[2,2,256,1024]{3,2,1,0:T(8,128)} reshape(f32[2,2,2,128,8,128]{5,4,3,2,1,0:T(8,128)} %bitcast.461) | data formatting | bytes 8388608 | tf_op jit(solution)/shard_map/reshape | solution.py:122
  22.2 32.6 %collective-permute-done = f32[16,2,2,128,128]{4,3,2,1,0:T(8,128)} collective-permute-done((f32[16,2,2,128,128]{4,3,2,1,0:T(8,128)}, f32[16,2,2,128,128]{4,3,2,1,0:T(8,128)}, u32[]{:S(2)}, u32[]{:S(2)}) %collective-permute-start) | collective-permute-done | bytes 4194336 | tf_op jit(solution)/shard_map/ppermute | solution.py:17
  54.8 6.6 %copy.112 = f32[2,8,2,2,128,128]{5,1,4,0,3,2:T(8,128)} copy(f32[2,8,2,2,128,128]{5,4,3,2,1,0:T(8,128)} %bitcast.6) | data formatting | bytes 8388608 | tf_op jit(solution)/shard_map/reshape | solution.py:119
  61.3 4.9 reshape.52
  66.2 8.3 %pad_maximum_fusion = f32[2,2,512,1024]{3,2,1,0:T(8,128)} fusion(f32[2,2,256,1024]{3,2,1,0:T(8,128)} %reshape.52, f32[2,2,256,1024]{3,2,1,0:T(8,128)} %reshape.50), kind=kLoop, calls=%fused_computation.377 | loop fusion | flops 2097152 | bytes 16777216 | tf_op jit(solution)/shard_map/concatenate | solution.py:139
  74.6 4.3 broadcast_in_dim.2
  78.9 93.1 %while.12 = (s32[]{:T(128)}, f32[2,2,512,1024]{3,2,1,0:T(8,128)}, s32[]{:T(128)}, s32[2]{0:T(128)S(1)}, s32[]{:T(128)}, /*index=5*/s32[2]{0:T(128)S(1)}, f32[4,2...) while((s32[]{:T(128)}, f32[2,2,512,1024]{3,2,1,0:T(8,128)}, ...), condition=%wide.region_6.7_spmd.clone.clone, body=%wide.region_0.6_spmd.clone.clone.sunk | while | flops 6523715584 | bytes 125305184 | solution.py:164
  83.8 1.7 dynamic-slice_bitcast_fusion.5
  94.7 2.5 subtract_convert_fusion.7
  124.1 1.7 fusion.653
  128.3 1.9 subtract_convert_fusion.9
  139.2 2.4 add_convert_fusion.5
  150.4 1.6 fusion.670
  152.1 1.8 maximum_add_fusion.2
  153.9 11.5 %dynamic_update_slice.6 = f32[2,2,512,1024]{3,2,1,0:T(8,128)} dynamic-update-slice(f32[2,2,512,1024]{3,2,1,0:T(8,128)} %get-tuple-element.510, f32[2,2,256,256]{3,2,1,0:T(8,128)S(1)} %maximum_add_fusion.2, s32[]{:T(128)} %constant.14.clone.1..sunk, s32[]{:T(128)} %constant.14.clone.1..sunk, s32[]{:T(128)S(6)} %select_n.300, s32[]{:T(128)S(6)} %select_n.301) | dynamic-update-slice | bytes 2097156 | tf_op jit(solution)/shard_map/while/body/dynamic_update_slice | solution.py:161
  172.0 5.5 %copy.109 = f32[256,8,8,128]{3,2,1,0:T(8,128)S(1)} copy(f32[256,8,8,128]{3,1,2,0:T(8,128)} %bitcast.455) | data formatting | bytes 16777216
  179.0 91.5 %collective-permute-start.1 = (f32[8192,128]{1,0:T(8,128)S(1)}, f32[8192,128]{1,0:T(8,128)S(1)}, u32[]{:S(2)}, u32[]{:S(2)}) collective-permute-start(f32[8192,128]{1,0:T(8,128)S(1)} %bitcast.464), channel_id=1, source_target_pairs={{0,4},{4,8},{8,12},{12,16},{16,20},{20,24},{24,28},{1,5},{5,9},{9,... | collective-permute-start | bytes 12582920 | tf_op jit(solution)/shard_map/ppermute | solution.py:17
  271.3 44.4 %collective-permute-done.1 = f32[8192,128]{1,0:T(8,128)S(1)} collective-permute-done((f32[8192,128]{1,0:T(8,128)S(1)}, f32[8192,128]{1,0:T(8,128)S(1)}, u32[]{:S(2)}, u32[]{:S(2)}) %collective-permute-start.1) | collective-permute-done | bytes 4194336 | tf_op jit(solution)/shard_map/ppermute | solution.py:17
  315.8 2.4 bitcast_add_fusion
  318.2 157.0 %all-reduce.2.cloned.1.call-done = f32[8192,128]{1,0:T(8,128)} async-done(((f32[8192,128]{1,0:T(8,128)}), f32[8192,128]{1,0:T(8,128)}) %all-reduce.2.cloned.1.call-update) | async-done | bytes 4194320 | tf_op jit(solution)/shard_map/psum | solution.py:173
  475.2 6.0 %bitcast_subtract_fusion.1 = f32[8192,128]{1,0:T(8,128)} fusion(f32[16,2,2,128,128]{4,3,2,1,0:T(8,128)} %param.9, f32[8192,128]{1,0:T(8,128)} %all-reduce.2.cloned.1.call-done), kind=kLoop, calls=%fused_computation.379 | loop fusion | flops 2097152 | bytes 12582912 | tf_op jit(solution)/shard_map/sub | solution.py:174
  (62 shorter events, 62.3 us)
Async XLA Ops:
  6.5 468.7 %all-reduce.2.cloned.1.call-start = ((), (), s32[]{:S(2)}) async-start(), calls=%async_computation | async-start | bytes 8388608 | tf_op jit(solution)/shard_map/psum | solution.py:173
  6.5 48.2 %collective-permute-start = (f32[16,2,2,128,128]{4,3,2,1,0:T(8,128)}, f32[16,2,2,128,128]{4,3,2,1,0:T(8,128)}, u32[]{:S(2)}, u32[]{:S(2)}) collective-permute-start(f32[16,2,2,128,128]{4,3,2,1,0:T(8,128)} %param.9), channel_id=1, source_target_pairs={{4,0},{8,4},{12,8},{16,12},{20,16},{24,20},{28,24},{5,1},{9,5},{13... | collective-permute-start | bytes 12582920 | tf_op jit(solution)/shard_map/ppermute | solution.py:17
  8.5 2.8 copy-start
  15.7 4.9 %copy-start.1 = (f32[256,256]{1,0:T(8,128)S(1)}, f32[256,256]{1,0:T(8,128)}, u32[]{:S(2)}) copy-start(f32[256,256]{1,0:T(8,128)} %param.11) | copy-start | bytes 786436
  74.6 4.3 copy-start.2
  74.6 4.3 copy-start.3
  179.0 136.7 %collective-permute-start.1 = (f32[8192,128]{1,0:T(8,128)S(1)}, f32[8192,128]{1,0:T(8,128)S(1)}, u32[]{:S(2)}, u32[]{:S(2)}) collective-permute-start(f32[8192,128]{1,0:T(8,128)S(1)} %bitcast.464), channel_id=1, source_target_pairs={{0,4},{4,8},{8,12},{12,16},{16,20},{20,24},{24,28},{1,5},{5,9},{9,... | collective-permute-start | bytes 12582920 | tf_op jit(solution)/shard_map/ppermute | solution.py:17
Sparse Core Ops, SparseCore 0:
  318.3 156.8 all-reduce.1
where the time goes:
time: 497 us; the launch traced here: 488 us
  waiting for transfers between devices  234 us (47%)
  starting transfers between devices  93.4 us (19%)
  matrix products  64.9 us (13%)
  local copies, waits for them, and re-layouts  51.8 us (10%)
  other arithmetic  19.9 us (4%)
  between operations  13.7 us (3%)
  loops' own time  10.6 us (2%)
    psum x1, waiting for transfers between devices, per_device(): combined = lax.psum(own_rows + arrived, 'pos')  157 us
    ppermute x2, starting transfers between devices, shifted(): return lax.ppermute(shard, axis, pairs)  93.4 us
    ppermute x2, waiting for transfers between devices, shifted(): return lax.ppermute(shard, axis, pairs)  77 us
    dot_general x24, matrix products, right_product(): jnp.einsum('mjk,kl->mjl', field, matrix, preferred_element_type=jnp.float32)  34.4 us
    dot_general x24, matrix products, left_product(): jnp.einsum('jk,mkl->mjl', matrix, field, preferred_element_type=jnp.float32)  30.5 us
    dynamic_update_slice x1, local copies, waits for them, and re-layouts, one_position(): return lax.dynamic_update_slice(gradient, former + term, corner)  11.5 us
    reshape x2, local copies, waits for them, and re-layouts, tiles_to_band(): tiles.reshape(band_tiles, across, slice_count, 2, tile_side, tile_side)  11 us
    another operation x1, loops' own time, per_device(): gradient = lax.fori_loop(0, live_count, one_position, empty)  10.6 us
  transfers between devices with their start and end apart: 3, of which 3 were waited for; matrix products, arithmetic and copies ran while one was open for 3% of the time, Pallas kernels for 0%

commit v1 on v0

v1 whole, which is shorter than its diff:
```python
import functools
import math

import jax
import jax.numpy as jnp
from jax import lax
from jax.experimental import pallas as pl
from jax.experimental.pallas import tpu as pltpu
from jax.sharding import PartitionSpec as P

TGX = 8
LANES = 128

step_size = 0.05


def shifted(shard, axis, by):
    count = lax.axis_size(axis)
    pairs = [(i, i + by) for i in range(count) if 0 <= i + by < count]
    return lax.ppermute(shard, axis, pairs)


def rotated(shard, axis, by):
    count = lax.axis_size(axis)
    return lax.ppermute(shard, axis, [(i, (i + by) % count) for i in range(count)])


def make_tables(length):
    counter = jnp.arange(length, dtype=jnp.int32)
    product = counter[:, None] * counter[None, :] % length
    angles = product.astype(jnp.float32) * jnp.float32(2.0 * math.pi / length)
    factor = jnp.float32(1.0 / math.sqrt(length))
    return (
        (jnp.cos(angles) * factor).astype(jnp.bfloat16),
        (jnp.sin(angles) * factor).astype(jnp.bfloat16),
    )


def make_matrices(length):
    cos_table, sin_table = make_tables(length)
    plus = jnp.concatenate(
        [
            jnp.concatenate([cos_table, -sin_table], axis=1),
            jnp.concatenate([sin_table, cos_table], axis=1),
        ],
        axis=0,
    )
    minus = jnp.concatenate(
        [
            jnp.concatenate([cos_table, sin_table], axis=1),
            jnp.concatenate([-sin_table, cos_table], axis=1),
        ],
        axis=0,
    )
    return jnp.stack([plus, minus])


def full_spec():
    return pl.BlockSpec(memory_space=pltpu.VMEM)


def scalar_spec():
    return pl.BlockSpec(memory_space=pltpu.SMEM)


def store_columns(tiles_ref, base, component, column, write):
    first = column // LANES
    shift = column % LANES
    back = (LANES - shift) % LANES
    third = jnp.minimum(first + 2, TGX - 1)
    left = pltpu.roll(tiles_ref[base + first, component], back, 1)
    middle = pltpu.roll(tiles_ref[base + first + 1, component], back, 1)
    right = pltpu.roll(tiles_ref[base + third, component], back, 1)
    lane = lax.broadcasted_iota(jnp.int32, left.shape, 1)
    keep = lane < LANES - shift
    write(0, jnp.where(keep, left, middle))
    write(1, jnp.where(keep, middle, right))


def window_kernel(column_ref, tiles_ref, out_ref):
    slots = out_ref.shape[0]
    components = tiles_ref.shape[1]
    side = tiles_ref.shape[2]
    rows = tiles_ref.shape[0] // TGX
    for slot in range(slots):
        column = column_ref[slot]

        def body(component, carry):
            for row in range(rows):

                def write(half, value):
                    out_ref[
                        slot, component, row * side : (row + 1) * side, half * LANES : (half + 1) * LANES
                    ] = value

                store_columns(tiles_ref, row * TGX, component, column, write)
            return carry

        lax.fori_loop(0, components, body, 0)


def column_windows(columns, tiles, pixels):
    band = tiles.shape[0] // TGX * tiles.shape[2]
    return pl.pallas_call(
        window_kernel,
        out_shape=jax.ShapeDtypeStruct((columns.shape[0], tiles.shape[1], band, pixels), jnp.float32),
        in_specs=[scalar_spec(), full_spec()],
        out_specs=full_spec(),
        compiler_params=pltpu.CompilerParams(vmem_limit_bytes=32 * 1024 * 1024),
    )(columns, tiles)


def position_kernel(
    place_ref,
    tiles_ref,
    halo_ref,
    probe_ref,
    wave_ref,
    measured_ref,
    matrix_ref,
    out_ref,
    canvas,
    patch,
    field,
    far,
    intensity,
):
    row = place_ref[0]
    column = place_ref[1]
    live = place_ref[2]
    components, pixels = patch.shape[0], patch.shape[1]
    modes = probe_ref.shape[0]
    side = tiles_ref.shape[2]
    band_tiles = tiles_ref.shape[0] // TGX
    band_rows = band_tiles * side
    plus, minus = 0, 1

    def fill(component, carry):
        for tile_row in range(band_tiles):

            def write(half, value):
                canvas[component, half, tile_row * side : (tile_row + 1) * side, :] = value

            store_columns(tiles_ref, tile_row * TGX, component, column, write)
        for half in range(pixels // LANES):
            lanes = slice(half * LANES, (half + 1) * LANES)
            canvas[component, half, band_rows:, :] = halo_ref[component, :, lanes]
            patch[component, :, lanes] = canvas[component, half, pl.ds(row, pixels), :]
        return carry

    lax.fori_loop(0, components, fill, 0)

    def transform(real, imag, left, right):
        stacked = jnp.concatenate([real, imag], axis=0).astype(jnp.bfloat16)
        upper = jnp.dot(matrix_ref[left], stacked, preferred_element_type=jnp.float32)
        upper = upper.astype(jnp.bfloat16)
        upper = jnp.concatenate([upper[:pixels], upper[pixels:]], axis=1)
        return jnp.dot(upper, matrix_ref[right], preferred_element_type=jnp.float32)

    def forward_transform(real, imag):
        return transform(real, imag, minus, plus)

    def inverse_transform(real, imag):
        return transform(real, imag, plus, minus)

    intensity[...] = jnp.zeros_like(intensity)

    def forward(mode, carry):
        field_re, field_im = probe_ref[mode, 0], probe_ref[mode, 1]
        spec = forward_transform(
            field_re * patch[0] - field_im * patch[1],
            field_re * patch[1] + field_im * patch[0],
        )
        spec_re, spec_im = spec[:, :pixels], spec[:, pixels:]
        moved = inverse_transform(
            wave_ref[0] * spec_re - wave_ref[1] * spec_im,
            wave_ref[0] * spec_im + wave_ref[1] * spec_re,
        )
        field[mode] = moved
        field_re, field_im = moved[:, :pixels], moved[:, pixels:]
        psi = forward_transform(
            field_re * patch[2] - field_im * patch[3],
            field_re * patch[3] + field_im * patch[2],
        )
        far[mode] = psi
        psi_re, psi_im = psi[:, :pixels], psi[:, pixels:]
        intensity[...] += psi_re * psi_re + psi_im * psi_im
        return carry

    lax.fori_loop(0, modes, forward, 0, unroll=2)

    intensity[...] -= measured_ref[...]
    out_ref[...] = jnp.zeros_like(out_ref)

    def backward(mode, carry):
        misfit = intensity[...]
        psi = far[mode]
        back = inverse_transform(misfit * psi[:, :pixels], misfit * psi[:, pixels:])
        back_re, back_im = back[:, :pixels], back[:, pixels:]
        field_re, field_im = field[mode, :, :pixels], field[mode, :, pixels:]
        out_ref[2] += field_re * back_re + field_im * back_im
        out_ref[3] += field_re * back_im - field_im * back_re
        spec = forward_transform(
            patch[2] * back_re + patch[3] * back_im,
            patch[2] * back_im - patch[3] * back_re,
        )
        spec_re, spec_im = spec[:, :pixels], spec[:, pixels:]
        back = inverse_transform(
            wave_ref[0] * spec_re + wave_ref[1] * spec_im,
            wave_ref[0] * spec_im - wave_ref[1] * spec_re,
        )
        back_re, back_im = back[:, :pixels], back[:, pixels:]
        field_re, field_im = probe_ref[mode, 0], probe_ref[mode, 1]
        out_ref[0] += field_re * back_re + field_im * back_im
        out_ref[1] += field_re * back_im - field_im * back_re
        return carry

    lax.fori_loop(0, modes, backward, 0, unroll=2)

    @pl.when(live == 0)
    def _():
        out_ref[...] = jnp.zeros_like(out_ref)


def position_gradient(place, tiles, halo, probe, wave, measured, matrices):
    components = tiles.shape[1]
    modes, _, pixels, _ = probe.shape
    band_rows = tiles.shape[0] // TGX * tiles.shape[2]
    products = 6 * modes * 2 * 2 * (2 * pixels) ** 2 * pixels
    return pl.pallas_call(
        position_kernel,
        out_shape=jax.ShapeDtypeStruct((components, pixels, pixels), jnp.float32),
        in_specs=[scalar_spec()] + [full_spec()] * 6,
        out_specs=full_spec(),
        scratch_shapes=[
            pltpu.VMEM((components, pixels // LANES, 2 * band_rows, LANES), jnp.float32),
            pltpu.VMEM((components, pixels, pixels), jnp.float32),
            pltpu.VMEM((modes, pixels, 2 * pixels), jnp.float32),
            pltpu.VMEM((modes, pixels, 2 * pixels), jnp.float32),
            pltpu.VMEM((pixels, pixels), jnp.float32),
        ],
        cost_estimate=pl.CostEstimate(flops=products, bytes_accessed=12 * 2**20, transcendentals=0),
        compiler_params=pltpu.CompilerParams(vmem_limit_bytes=48 * 1024 * 1024),
    )(place, tiles, halo, probe, wave, measured, matrices)


def scatter_kernel(row_ref, column_ref, patch_ref, own_ref, spill_ref, canvas):
    count, pixels = patch_ref.shape[0], patch_ref.shape[1]
    band_rows = own_ref.shape[1]
    canvas[...] = jnp.zeros_like(canvas)

    def body(index, carry):
        row = row_ref[index]
        column = column_ref[index]
        first = column // LANES
        shift = column % LANES
        left = pltpu.roll(patch_ref[index, :, :LANES], shift, 1)
        right = pltpu.roll(patch_ref[index, :, LANES:], shift, 1)
        lane = lax.broadcasted_iota(jnp.int32, left.shape, 1)
        late = lane >= shift
        zero = jnp.zeros_like(left)
        rows = pl.ds(row, pixels)
        canvas[first, rows, :] += jnp.where(late, left, zero)
        canvas[first + 1, rows, :] += jnp.where(late, right, left)
        canvas[first + 2, rows, :] += jnp.where(late, zero, right)
        return carry

    lax.fori_loop(0, count, body, 0)
    tiles = own_ref.shape[0]
    own_ref[...] = canvas[:tiles, :band_rows, :]
    spill_ref[...] = canvas[:tiles, band_rows:, :]


def scatter(rows, columns, patches, band_rows):
    shape = jax.ShapeDtypeStruct((TGX, band_rows, LANES), jnp.float32)
    return pl.pallas_call(
        scatter_kernel,
        out_shape=(shape, shape),
        in_specs=[scalar_spec(), scalar_spec(), full_spec()],
        out_specs=(full_spec(), full_spec()),
        scratch_shapes=[pltpu.VMEM((TGX + 1, 2 * band_rows, LANES), jnp.float32)],
        compiler_params=pltpu.CompilerParams(vmem_limit_bytes=32 * 1024 * 1024),
    )(rows, columns, patches)


def dense_update(object_tiles, gradients, rows, columns, band_rows):
    _, slices, _, side, _ = object_tiles.shape
    components, pixels = gradients[0].shape[0], gradients[0].shape[1]
    band_tiles = band_rows // side
    canvas = jnp.zeros((components, 2 * band_rows, TGX * side), jnp.float32)
    zero = jnp.int32(0)
    for slot, gradient in enumerate(gradients):
        corner = (zero, rows[slot], columns[slot])
        former = lax.dynamic_slice(canvas, corner, gradient.shape)
        canvas = lax.dynamic_update_slice(canvas, former + gradient, corner)
    shaped = canvas.reshape(components, 2, band_tiles, side, TGX, side).transpose(1, 2, 4, 0, 3, 5)
    shaped = shaped.reshape(2, -1, side)
    combined = lax.psum(shaped[0] + shifted(shaped[1], "region", 1), "pos")
    return object_tiles - step_size * combined.reshape(object_tiles.shape)


def per_device(object_tiles, probe, fresnel_phase, patterns, row_offsets, col_offsets, counts):
    slots = patterns.shape[2]
    pixels = patterns.shape[-1]
    held, slices, _, side, _ = object_tiles.shape
    components = 2 * slices
    band_tiles = held // TGX
    band_rows = band_tiles * side
    groups = lax.axis_size("pos")
    me = lax.axis_index("pos")
    tiles = object_tiles.reshape(held, components, side, side)
    measured = patterns.reshape(slots, pixels, pixels)
    rows = row_offsets.reshape(slots) - lax.axis_index("region") * band_rows
    columns = col_offsets.reshape(slots)
    live = (jnp.arange(slots, dtype=jnp.int32) < counts.reshape(())).astype(jnp.int32)

    wanted = shifted(columns, "region", 1)
    windows = column_windows(wanted, tiles, pixels)
    halos = [shifted(windows[slot], "region", -1) for slot in range(slots)]

    matrices = make_matrices(pixels)
    wave = jnp.stack([jnp.cos(fresnel_phase), jnp.sin(fresnel_phase)])
    places = jnp.stack([rows, columns, live], axis=1)

    gradients = [
        position_gradient(places[slot], tiles, halos[slot], probe, wave, measured[slot], matrices)
        for slot in range(slots)
    ]
    if groups != components:
        return dense_update(object_tiles, gradients, rows, columns, band_rows)

    corner = jnp.stack([rows, columns])
    corners = [corner] + [rotated(corner, "pos", by) for by in range(1, groups)]
    parts = []
    for gradient in gradients:
        for by in range(groups):
            piece = lax.dynamic_index_in_dim(gradient, lax.rem(me + by, groups), 0, keepdims=False)
            parts.append(piece if by == 0 else rotated(piece, "pos", by))
    all_rows = jnp.stack([corners[by][0, slot] for slot in range(slots) for by in range(groups)])
    all_columns = jnp.stack([corners[by][1, slot] for slot in range(slots) for by in range(groups)])
    own, spill = scatter(all_rows, all_columns, jnp.stack(parts), band_rows)
    arrived = shifted(spill, "region", 1)
    total = (own + arrived).reshape(TGX, band_tiles, side, side).transpose(1, 0, 2, 3)
    total = total.reshape(held, side, side)
    mine = lax.dynamic_index_in_dim(tiles, me, 1, keepdims=False) - step_size * total

    rightward, leftward = [mine], [mine]
    for _ in range(groups - 1):
        rightward.append(shifted(rightward[-1], "pos", 1))
        leftward.append(shifted(leftward[-1], "pos", -1))
    found = [mine] + [leftward[by] + rightward[groups - by] for by in range(1, groups)]
    result = jnp.zeros_like(tiles)
    for by in range(groups):
        result = lax.dynamic_update_slice_in_dim(
            result, found[by][:, None], lax.rem(me + by, groups), 1
        )
    return result.reshape(object_tiles.shape)


def solution(mesh):
    in_specs = (
        P("region", None, None, None, None),
        P(),
        P(),
        P("region", "pos", None, None, None),
        P("region", "pos", None),
        P("region", "pos", None),
        P("region", "pos"),
    )
    out_specs = P("region", None, None, None, None)
    return jax.shard_map(
        per_device, mesh=mesh, in_specs=in_specs, out_specs=out_specs, check_vma=False
    )
```

time: 497 us -> 213 us (0.43); the launches traced: 488 us -> 212 us
  waiting for transfers between devices: 234 us -> 103 us
  matrix products: 64.9 us -> 0 us
  starting transfers between devices: 93.4 us -> 39.3 us
  Pallas kernels: 0 us -> 40.8 us
  local copies, waits for them, and re-layouts: 51.8 us -> 22.3 us
  other arithmetic: 19.9 us -> 5.11 us
  between operations: 13.7 us -> 1.02 us
  loops' own time: 10.6 us -> 0 us
    psum x1 -> x0, waiting for transfers between devices: 157 us -> none  [per_device(): combined = lax.psum(own_rows + arrived, 'pos')]
    ppermute x2 -> x10, starting transfers between devices: 93.4 us -> 24.9 us  [shifted(): return lax.ppermute(shard, axis, pairs)]
    dot_general x48 -> x0, matrix products: 64.9 us -> none  [the longest x24 34.4 us: right_product(): jnp.einsum('mjk,kl->mjl', field, matrix, preferred_element_type=jnp.float32)]
    pallas_call x0 -> x4, Pallas kernels: none -> 40.8 us  [the longest x2 36 us: position_gradient(): pl.pallas_call(position_kernel, out_shape=jax.ShapeDtypeStruct((component...]
    reshape x4 -> x0, local copies, waits for them, and re-layouts: 20.8 us -> none  [the longest x2 11 us: tiles_to_band(): tiles.reshape(band_tiles, across, slice_count, 2, tile_side, tile_side)]
    ppermute x0 -> x9, waiting for transfers between devices: none -> 17.6 us  [rotated(): lax.ppermute(shard, axis, [(i, (i + by) % count) for i in range(count)])]
    ppermute x0 -> x9, starting transfers between devices: none -> 14.4 us  [rotated(): lax.ppermute(shard, axis, [(i, (i + by) % count) for i in range(count)])]
    dynamic_update_slice x1 -> x0, local copies, waits for them, and re-layouts: 11.5 us -> none  [one_position(): return lax.dynamic_update_slice(gradient, former + term, corner)]
  transfers between devices with their start and end apart: 3 -> 19, of which waited for: 3 -> 9; matrix products, arithmetic and copies ran while one was open for 3% -> 9% of each run, Pallas kernels for 0% -> 18%
where the time goes in v1:
time: 213 us; the launch traced here: 212 us
  waiting for transfers between devices  103 us (48%)
  Pallas kernels  40.8 us (19%)
  starting transfers between devices  39.3 us (18%)
  local copies, waits for them, and re-layouts  22.3 us (10%)
  other arithmetic  5.11 us (2%)
    ppermute x10, waiting for transfers between devices, shifted(): return lax.ppermute(shard, axis, pairs)  85.7 us
    pallas_call x2, Pallas kernels, position_gradient(): pl.pallas_call(position_kernel, out_shape=jax.ShapeDtypeStruct((component...  36 us
    ppermute x10, starting transfers between devices, shifted(): return lax.ppermute(shard, axis, pairs)  24.9 us
    ppermute x9, waiting for transfers between devices, rotated(): lax.ppermute(shard, axis, [(i, (i + by) % count) for i in range(count)])  17.6 us
    ppermute x9, starting transfers between devices, rotated(): lax.ppermute(shard, axis, [(i, (i + by) % count) for i in range(count)])  14.4 us
    unnamed x19, local copies, waits for them, and re-layouts  6.28 us
    another operation x1, local copies, waits for them, and re-layouts, per_device(): jnp.stack([corners[by][1, slot] for slot in range(slots) for by in range(...  5.03 us
    another operation x1, local copies, waits for them, and re-layouts, per_device(): jnp.stack([corners[by][0, slot] for slot in range(slots) for by in range(...  4.98 us
  transfers between devices with their start and end apart: 19, of which 9 were waited for; matrix products, arithmetic and copies ran while one was open for 9% of the time, Pallas kernels for 18%

profile of v1, /device:TPU:2, one launch (start us, length us, event | category | flops | bytes accessed | tf_op | source)
XLA Modules:
  0.0 211.9 jit_solution(10158257910875356136)
XLA Ops:
  2.9 2.6 %collective-permute-start.1 = (s32[2,2]{1,0:T(2,128)S(1)}, s32[2,2]{1,0:T(2,128)S(1)}, u32[]{:S(2)}, u32[]{:S(2)}) collective-permute-start(s32[2,2]{1,0:T(2,128)S(1)} %pad_add_fusion.1), channel_id=1, source_target_pairs={{0,2},{1,3},{2,0},{3,1},{4,6},{5,7},{6,4},{7,5},{8,10},{9,11},{10,... | collective-permute-start | bytes 56 | tf_op jit(solution)/shard_map/ppermute | solution.py:25
  12.4 2.2 %copy-done = f32[16,2,2,128,128]{4,3,2,1,0:T(8,128)S(1)} copy-done((f32[16,2,2,128,128]{4,3,2,1,0:T(8,128)S(1)}, f32[16,2,2,128,128]{4,3,2,1,0:T(8,128)}, u32[]{:S(2)}) %copy-start) | copy-done | bytes 4194328
  17.6 3.6 %collective-permute-start.4 = (f32[4,256,256]{2,1,0:T(8,128)}, f32[4,256,256]{2,1,0:T(8,128)S(1)}, u32[]{:S(2)}, u32[]{:S(2)}) collective-permute-start(f32[4,256,256]{2,1,0:T(8,128)} %get-tuple-element.12), channel_id=1, source_target_pairs={{4,0},{8,4},{12,8},{16,12},{20,16},{24,20},{28,24},{5,1},{9,5},{13... | collective-permute-start | bytes 3145736 | tf_op jit(solution)/shard_map/ppermute | solution.py:20
  23.1 2.1 collective-permute-start.8
  25.8 8.1 %collective-permute-done.4.halo_ref = f32[4,256,256]{2,1,0:T(8,128)S(1)} collective-permute-done((f32[4,256,256]{2,1,0:T(8,128)}, f32[4,256,256]{2,1,0:T(8,128)S(1)}, u32[]{:S(2)}, u32[]{:S(2)}) %collective-permute-start.4) | collective-permute-done | bytes 1048608 | tf_op jit(solution)/shard_map/ppermute | solution.py:20
  33.9 18.0 %shard_map.74 = f32[4,256,256]{2,1,0:T(8,128)S(1)} custom-call(s32[3]{0:T(128)S(1)} %get-tuple-element.10.place_ref, f32[16,4,128,128]{3,2,1,0:T(8,128)} %bitcast.89, f32[4,256,256]{2,1,0:T(8,128)S(1)} %collective-permute-done.4.halo_ref, f32[4,2,256,256]{3,2,1,0:T(8,128)S(1)} %copy-done.2, f32[2,256,256]{2,1,0:T(8,128)S(1)} %pad_maximum_fusion.5.wave_ref, ...), custom_call_target="tpu_custom_call" | custom-call | flops 6442450944 | bytes 12582912 | tf_op jit(solution)/shard_map/pallas_call | solution.py:230
  53.2 18.0 %shard_map.75 = f32[4,256,256]{2,1,0:T(8,128)S(1)} custom-call(s32[3]{0:T(128)S(1)} %get-tuple-element.9.place_ref, f32[16,4,128,128]{3,2,1,0:T(8,128)} %bitcast.90, f32[4,256,256]{2,1,0:T(8,128)S(1)} %collective-permute-done.8.halo_ref, f32[4,2,256,256]{3,2,1,0:T(8,128)S(1)} %copy-done.2, f32[2,256,256]{2,1,0:T(8,128)S(1)} %pad_maximum_fusion.5.wave_ref, ...), custom_call_target="tpu_custom_call" | custom-call | flops 6442450944 | bytes 12582912 | tf_op jit(solution)/shard_map/pallas_call | solution.py:230
  71.3 2.9 %collective-permute-start.7 = (f32[256,256]{1,0:T(8,128)S(1)}, f32[256,256]{1,0:T(8,128)S(1)}, u32[]{:S(2)}, u32[]{:S(2)}) collective-permute-start(f32[256,256]{1,0:T(8,128)S(1)} %get-tuple-element.17), channel_id=1, source_target_pairs={{0,3},{1,0},{2,1},{3,2},{4,7},{5,4},{6,5},{7,6},{8,11},{9,8},{10,9... | collective-permute-start | bytes 786440 | tf_op jit(solution)/shard_map/ppermute | solution.py:25
  74.2 6.3 %collective-permute-done.7 = f32[256,256]{1,0:T(8,128)S(1)} collective-permute-done((f32[256,256]{1,0:T(8,128)S(1)}, f32[256,256]{1,0:T(8,128)S(1)}, u32[]{:S(2)}, u32[]{:S(2)}) %collective-permute-start.7) | collective-permute-done | bytes 262176 | tf_op jit(solution)/shard_map/ppermute | solution.py:25
  80.6 2.4 %collective-permute-start.9 = (f32[256,256]{1,0:T(8,128)S(1)}, f32[256,256]{1,0:T(8,128)S(1)}, u32[]{:S(2)}, u32[]{:S(2)}) collective-permute-start(f32[256,256]{1,0:T(8,128)S(1)} %get-tuple-element.15), channel_id=1, source_target_pairs={{0,1},{1,2},{2,3},{3,0},{4,5},{5,6},{6,7},{7,4},{8,9},{9,10},{10,1... | collective-permute-start | bytes 786440 | tf_op jit(solution)/shard_map/ppermute | solution.py:25
  86.3 5.0 %stack.57.row_ref = s32[8]{0:T(128)S(1)} concatenate(s32[1]{0:T(128)} %bitcast.2, s32[1]{0:T(128)} %bitcast.4, s32[1]{0:T(128)} %bitcast.5, s32[1]{0:T(128)} %bitcast.6, s32[1]{0:T(128)} %bitcast.7, s32[1]{0:T(128)} %bitcast.8, s32[1]{0:T(128)} %bitcast.9, s32[1]{0:T(128)} %bitcast.10), dimensions={0} | concatenate | bytes 64 | tf_op jit(solution)/shard_map/stack | solution.py:339
  91.3 5.0 %stack.58.column_ref = s32[8]{0:T(128)S(1)} concatenate(s32[1]{0:T(128)} %bitcast.11, s32[1]{0:T(128)} %bitcast.12, s32[1]{0:T(128)} %bitcast.13, s32[1]{0:T(128)} %bitcast.14, s32[1]{0:T(128)} %bitcast.15, s32[1]{0:T(128)} %bitcast.16, s32[1]{0:T(128)} %bitcast.17, s32[1]{0:T(128)} %bitcast.18), dimensions={0} | concatenate | bytes 64 | tf_op jit(solution)/shard_map/stack | solution.py:340
  97.2 5.8 %collective-permute-done.10 = f32[256,256]{1,0:T(8,128)S(1)} collective-permute-done((f32[256,256]{1,0:T(8,128)S(1)}, f32[256,256]{1,0:T(8,128)S(1)}, u32[]{:S(2)}, u32[]{:S(2)}) %collective-permute-start.10) | collective-permute-done | bytes 262176 | tf_op jit(solution)/shard_map/ppermute | solution.py:25
  103.0 5.5 %collective-permute-done.11 = f32[256,256]{1,0:T(8,128)S(1)} collective-permute-done((f32[256,256]{1,0:T(8,128)S(1)}, f32[256,256]{1,0:T(8,128)S(1)}, u32[]{:S(2)}, u32[]{:S(2)}) %collective-permute-start.11) | collective-permute-done | bytes 262176 | tf_op jit(solution)/shard_map/ppermute | solution.py:25
  108.5 2.9 %shard_map.76 = (f32[8,256,128]{2,1,0:T(8,128)S(1)}, f32[8,256,128]{2,1,0:T(8,128)}) custom-call(s32[8]{0:T(128)S(1)} %stack.57.row_ref, s32[8]{0:T(128)S(1)} %stack.58.column_ref, f32[8,256,256]{2,1,0:T(8,128)S(1)} %bitcast_dynamic-update-slice_fusion.3.patch_ref), custom_call_target="tpu_custom_call" | custom-call | tf_op jit(solution)/shard_map/pallas_call | solution.py:276
  113.4 14.3 %collective-permute-done.12 = f32[8,256,128]{2,1,0:T(8,128)S(1)} collective-permute-done((f32[8,256,128]{2,1,0:T(8,128)}, f32[8,256,128]{2,1,0:T(8,128)S(1)}, u32[]{:S(2)}, u32[]{:S(2)}) %collective-permute-start.12) | collective-permute-done | bytes 1048608 | tf_op jit(solution)/shard_map/ppermute | solution.py:20
  130.1 2.6 %collective-permute-start.14 = (f32[16,128,128]{2,1,0:T(8,128)S(1)}, f32[16,128,128]{2,1,0:T(8,128)S(1)}, u32[]{:S(2)}, u32[]{:S(2)}) collective-permute-start(f32[16,128,128]{2,1,0:T(8,128)S(1)} %bitcast_subtract_fusion), channel_id=1, source_target_pairs={{0,1},{1,2},{2,3},{4,5},{5,6},{6,7},{8,9},{9,10},{10,11},{12,13},{... | collective-permute-start | bytes 3145736 | tf_op jit(solution)/shard_map/ppermute | solution.py:20
  134.0 20.9 %collective-permute-done.14 = f32[16,128,128]{2,1,0:T(8,128)S(1)} collective-permute-done((f32[16,128,128]{2,1,0:T(8,128)S(1)}, f32[16,128,128]{2,1,0:T(8,128)S(1)}, u32[]{:S(2)}, u32[]{:S(2)}) %collective-permute-start.14) | collective-permute-done | bytes 1048608 | tf_op jit(solution)/shard_map/ppermute | solution.py:20
  154.9 4.4 %collective-permute-start.15 = (f32[16,128,128]{2,1,0:T(8,128)S(1)}, f32[16,128,128]{2,1,0:T(8,128)S(1)}, u32[]{:S(2)}, u32[]{:S(2)}) collective-permute-start(f32[16,128,128]{2,1,0:T(8,128)S(1)} %collective-permute-done.14), channel_id=1, source_target_pairs={{0,1},{1,2},{2,3},{4,5},{5,6},{6,7},{8,9},{9,10},{10,11},{12,13},{... | collective-permute-start | bytes 3145736 | tf_op jit(solution)/shard_map/ppermute | solution.py:20
  160.6 20.0 %collective-permute-done.15 = f32[16,128,128]{2,1,0:T(8,128)S(1)} collective-permute-done((f32[16,128,128]{2,1,0:T(8,128)S(1)}, f32[16,128,128]{2,1,0:T(8,128)S(1)}, u32[]{:S(2)}, u32[]{:S(2)}) %collective-permute-start.15) | collective-permute-done | bytes 1048608 | tf_op jit(solution)/shard_map/ppermute | solution.py:20
  180.7 4.4 %collective-permute-start.16 = (f32[16,128,128]{2,1,0:T(8,128)S(1)}, f32[16,128,128]{2,1,0:T(8,128)S(1)}, u32[]{:S(2)}, u32[]{:S(2)}) collective-permute-start(f32[16,128,128]{2,1,0:T(8,128)S(1)} %collective-permute-done.15), channel_id=1, source_target_pairs={{0,1},{1,2},{2,3},{4,5},{5,6},{6,7},{8,9},{9,10},{10,11},{12,13},{... | collective-permute-start | bytes 3145736 | tf_op jit(solution)/shard_map/ppermute | solution.py:20
  187.1 18.5 %collective-permute-done.16 = f32[16,128,128]{2,1,0:T(8,128)S(1)} collective-permute-done((f32[16,128,128]{2,1,0:T(8,128)S(1)}, f32[16,128,128]{2,1,0:T(8,128)S(1)}, u32[]{:S(2)}, u32[]{:S(2)}) %collective-permute-start.16) | collective-permute-done | bytes 1048608 | tf_op jit(solution)/shard_map/ppermute | solution.py:20
  205.8 3.9 %collective-permute-done.18 = f32[16,128,128]{2,1,0:T(8,128)S(1)} collective-permute-done((f32[16,128,128]{2,1,0:T(8,128)S(1)}, f32[16,128,128]{2,1,0:T(8,128)S(1)}, u32[]{:S(2)}, u32[]{:S(2)}) %collective-permute-start.18) | collective-permute-done | bytes 1048608 | tf_op jit(solution)/shard_map/ppermute | solution.py:20
  209.9 2.0 copy-done.3
  (68 shorter events, 29.5 us)
Async XLA Ops:
  1.3 81.7 %collective-permute-start = (s32[2,2]{1,0:T(2,128)S(1)}, s32[2,2]{1,0:T(2,128)S(1)}, u32[]{:S(2)}, u32[]{:S(2)}) collective-permute-start(s32[2,2]{1,0:T(2,128)S(1)} %pad_add_fusion.1), channel_id=1, source_target_pairs={{0,1},{1,2},{2,3},{3,0},{4,5},{5,6},{6,7},{7,4},{8,9},{9,10},{10,1... | collective-permute-start | bytes 56 | tf_op jit(solution)/shard_map/ppermute | solution.py:25
  2.9 80.7 %collective-permute-start.1 = (s32[2,2]{1,0:T(2,128)S(1)}, s32[2,2]{1,0:T(2,128)S(1)}, u32[]{:S(2)}, u32[]{:S(2)}) collective-permute-start(s32[2,2]{1,0:T(2,128)S(1)} %pad_add_fusion.1), channel_id=1, source_target_pairs={{0,2},{1,3},{2,0},{3,1},{4,6},{5,7},{6,4},{7,5},{8,10},{9,11},{10,... | collective-permute-start | bytes 56 | tf_op jit(solution)/shard_map/ppermute | solution.py:25
  5.5 80.3 %collective-permute-start.2 = (s32[2,2]{1,0:T(2,128)S(1)}, s32[2,2]{1,0:T(2,128)S(1)}, u32[]{:S(2)}, u32[]{:S(2)}) collective-permute-start(s32[2,2]{1,0:T(2,128)S(1)} %pad_add_fusion.1), channel_id=1, source_target_pairs={{0,3},{1,0},{2,1},{3,2},{4,7},{5,4},{6,5},{7,6},{8,11},{9,8},{10,9... | collective-permute-start | bytes 56 | tf_op jit(solution)/shard_map/ppermute | solution.py:25
  6.8 5.6 %collective-permute-start.3 = (s32[2]{0:T(128)}, s32[2]{0:T(128)S(1)}, u32[]{:S(2)}, u32[]{:S(2)}) collective-permute-start(s32[2]{0:T(128)} %bitcast.96), channel_id=1, source_target_pairs={{0,4},{4,8},{8,12},{12,16},{16,20},{20,24},{24,28},{1,5},{5,9},{9,... | collective-permute-start | bytes 32 | tf_op jit(solution)/shard_map/ppermute | solution.py:20
  12.4 2.2 %copy-start = (f32[16,2,2,128,128]{4,3,2,1,0:T(8,128)S(1)}, f32[16,2,2,128,128]{4,3,2,1,0:T(8,128)}, u32[]{:S(2)}) copy-start(f32[16,2,2,128,128]{4,3,2,1,0:T(8,128)} %param.7) | copy-start | bytes 12582916
  16.5 5.4 %copy-start.5 = (f32[256,256]{1,0:T(8,128)S(1)}, f32[256,256]{1,0:T(8,128)}, u32[]{:S(2)}) copy-start(f32[256,256]{1,0:T(8,128)} %param.9) | copy-start | bytes 786436
  17.6 16.2 %collective-permute-start.4 = (f32[4,256,256]{2,1,0:T(8,128)}, f32[4,256,256]{2,1,0:T(8,128)S(1)}, u32[]{:S(2)}, u32[]{:S(2)}) collective-permute-start(f32[4,256,256]{2,1,0:T(8,128)} %get-tuple-element.12), channel_id=1, source_target_pairs={{4,0},{8,4},{12,8},{16,12},{20,16},{24,20},{28,24},{5,1},{9,5},{13... | collective-permute-start | bytes 3145736 | tf_op jit(solution)/shard_map/ppermute | solution.py:20
  22.9 2.3 %copy-start.6 = (s32[1,1,2]{2,1,0:T(1,128)S(1)}, s32[1,1,2]{2,1,0:T(1,128)}, u32[]{:S(2)}) copy-start(s32[1,1,2]{2,1,0:T(1,128)} %param.12) | copy-start | bytes 28
  22.9 2.9 %copy-start.4 = (f32[1,1,2,256,256]{4,3,2,1,0:T(8,128)S(1)}, f32[1,1,2,256,256]{4,3,2,1,0:T(8,128)}, u32[]{:S(2)}) copy-start(f32[1,1,2,256,256]{4,3,2,1,0:T(8,128)} %param.10) | copy-start | bytes 1572868
  22.9 11.0 %copy-start.2 = (f32[4,2,256,256]{3,2,1,0:T(8,128)S(1)}, f32[4,2,256,256]{3,2,1,0:T(8,128)}, u32[]{:S(2)}) copy-start(f32[4,2,256,256]{3,2,1,0:T(8,128)} %probe_ref.3) | copy-start | bytes 6291460
  23.1 29.7 %collective-permute-start.8 = (f32[4,256,256]{2,1,0:T(8,128)S(1)}, f32[4,256,256]{2,1,0:T(8,128)S(1)}, u32[]{:S(2)}, u32[]{:S(2)}) collective-permute-start(f32[4,256,256]{2,1,0:T(8,128)S(1)} %get-tuple-element.11), channel_id=1, source_target_pairs={{4,0},{8,4},{12,8},{16,12},{20,16},{24,20},{28,24},{5,1},{9,5},{13... | collective-permute-start | bytes 3145736 | tf_op jit(solution)/shard_map/ppermute | solution.py:20
  52.0 19.3 %collective-permute-start.5 = (f32[256,256]{1,0:T(8,128)S(1)}, f32[256,256]{1,0:T(8,128)S(1)}, u32[]{:S(2)}, u32[]{:S(2)}) collective-permute-start(f32[256,256]{1,0:T(8,128)S(1)} %get-tuple-element.19), channel_id=1, source_target_pairs={{0,1},{1,2},{2,3},{3,0},{4,5},{5,6},{6,7},{7,4},{8,9},{9,10},{10,1... | collective-permute-start | bytes 786440 | tf_op jit(solution)/shard_map/ppermute | solution.py:25
  52.9 21.3 %collective-permute-start.6 = (f32[256,256]{1,0:T(8,128)S(1)}, f32[256,256]{1,0:T(8,128)S(1)}, u32[]{:S(2)}, u32[]{:S(2)}) collective-permute-start(f32[256,256]{1,0:T(8,128)S(1)} %get-tuple-element.18), channel_id=1, source_target_pairs={{0,2},{1,3},{2,0},{3,1},{4,6},{5,7},{6,4},{7,5},{8,10},{9,11},{10,... | collective-permute-start | bytes 786440 | tf_op jit(solution)/shard_map/ppermute | solution.py:25
  71.3 9.2 %collective-permute-start.7 = (f32[256,256]{1,0:T(8,128)S(1)}, f32[256,256]{1,0:T(8,128)S(1)}, u32[]{:S(2)}, u32[]{:S(2)}) collective-permute-start(f32[256,256]{1,0:T(8,128)S(1)} %get-tuple-element.17), channel_id=1, source_target_pairs={{0,3},{1,0},{2,1},{3,2},{4,7},{5,4},{6,5},{7,6},{8,11},{9,8},{10,9... | collective-permute-start | bytes 786440 | tf_op jit(solution)/shard_map/ppermute | solution.py:25
  80.6 16.6 %collective-permute-start.9 = (f32[256,256]{1,0:T(8,128)S(1)}, f32[256,256]{1,0:T(8,128)S(1)}, u32[]{:S(2)}, u32[]{:S(2)}) collective-permute-start(f32[256,256]{1,0:T(8,128)S(1)} %get-tuple-element.15), channel_id=1, source_target_pairs={{0,1},{1,2},{2,3},{3,0},{4,5},{5,6},{6,7},{7,4},{8,9},{9,10},{10,1... | collective-permute-start | bytes 786440 | tf_op jit(solution)/shard_map/ppermute | solution.py:25
  84.2 18.8 %collective-permute-start.10 = (f32[256,256]{1,0:T(8,128)S(1)}, f32[256,256]{1,0:T(8,128)S(1)}, u32[]{:S(2)}, u32[]{:S(2)}) collective-permute-start(f32[256,256]{1,0:T(8,128)S(1)} %get-tuple-element.14), channel_id=1, source_target_pairs={{0,2},{1,3},{2,0},{3,1},{4,6},{5,7},{6,4},{7,5},{8,10},{9,11},{10,... | collective-permute-start | bytes 786440 | tf_op jit(solution)/shard_map/ppermute | solution.py:25
  96.4 12.1 %collective-permute-start.11 = (f32[256,256]{1,0:T(8,128)S(1)}, f32[256,256]{1,0:T(8,128)S(1)}, u32[]{:S(2)}, u32[]{:S(2)}) collective-permute-start(f32[256,256]{1,0:T(8,128)S(1)} %get-tuple-element.13), channel_id=1, source_target_pairs={{0,3},{1,0},{2,1},{3,2},{4,7},{5,4},{6,5},{7,6},{8,11},{9,8},{10,9... | collective-permute-start | bytes 786440 | tf_op jit(solution)/shard_map/ppermute | solution.py:25
  111.4 16.3 %collective-permute-start.12 = (f32[8,256,128]{2,1,0:T(8,128)}, f32[8,256,128]{2,1,0:T(8,128)S(1)}, u32[]{:S(2)}, u32[]{:S(2)}) collective-permute-start(f32[8,256,128]{2,1,0:T(8,128)} %get-tuple-element.8), channel_id=1, source_target_pairs={{0,4},{4,8},{8,12},{12,16},{16,20},{20,24},{24,28},{1,5},{5,9},{9,... | collective-permute-start | bytes 3145736 | tf_op jit(solution)/shard_map/ppermute | solution.py:20
  130.1 24.8 %collective-permute-start.14 = (f32[16,128,128]{2,1,0:T(8,128)S(1)}, f32[16,128,128]{2,1,0:T(8,128)S(1)}, u32[]{:S(2)}, u32[]{:S(2)}) collective-permute-start(f32[16,128,128]{2,1,0:T(8,128)S(1)} %bitcast_subtract_fusion), channel_id=1, source_target_pairs={{0,1},{1,2},{2,3},{4,5},{5,6},{6,7},{8,9},{9,10},{10,11},{12,13},{... | collective-permute-start | bytes 3145736 | tf_op jit(solution)/shard_map/ppermute | solution.py:20
  132.7 26.7 %collective-permute-start.13 = (f32[16,128,128]{2,1,0:T(8,128)S(1)}, f32[16,128,128]{2,1,0:T(8,128)S(1)}, u32[]{:S(2)}, u32[]{:S(2)}) collective-permute-start(f32[16,128,128]{2,1,0:T(8,128)S(1)} %bitcast_subtract_fusion), channel_id=1, source_target_pairs={{1,0},{2,1},{3,2},{5,4},{6,5},{7,6},{9,8},{10,9},{11,10},{13,12},{... | collective-permute-start | bytes 3145736 | tf_op jit(solution)/shard_map/ppermute | solution.py:20
  154.9 25.8 %collective-permute-start.15 = (f32[16,128,128]{2,1,0:T(8,128)S(1)}, f32[16,128,128]{2,1,0:T(8,128)S(1)}, u32[]{:S(2)}, u32[]{:S(2)}) collective-permute-start(f32[16,128,128]{2,1,0:T(8,128)S(1)} %collective-permute-done.14), channel_id=1, source_target_pairs={{0,1},{1,2},{2,3},{4,5},{5,6},{6,7},{8,9},{9,10},{10,11},{12,13},{... | collective-permute-start | bytes 3145736 | tf_op jit(solution)/shard_map/ppermute | solution.py:20
  159.3 25.8 %collective-permute-start.17 = (f32[16,128,128]{2,1,0:T(8,128)S(1)}, f32[16,128,128]{2,1,0:T(8,128)S(1)}, u32[]{:S(2)}, u32[]{:S(2)}) collective-permute-start(f32[16,128,128]{2,1,0:T(8,128)S(1)} %collective-permute-done.13), channel_id=1, source_target_pairs={{1,0},{2,1},{3,2},{5,4},{6,5},{7,6},{9,8},{10,9},{11,10},{13,12},{... | collective-permute-start | bytes 3145736 | tf_op jit(solution)/shard_map/ppermute | solution.py:20
  180.7 24.9 %collective-permute-start.16 = (f32[16,128,128]{2,1,0:T(8,128)S(1)}, f32[16,128,128]{2,1,0:T(8,128)S(1)}, u32[]{:S(2)}, u32[]{:S(2)}) collective-permute-start(f32[16,128,128]{2,1,0:T(8,128)S(1)} %collective-permute-done.15), channel_id=1, source_target_pairs={{0,1},{1,2},{2,3},{4,5},{5,6},{6,7},{8,9},{9,10},{10,11},{12,13},{... | collective-permute-start | bytes 3145736 | tf_op jit(solution)/shard_map/ppermute | solution.py:20
  185.1 24.6 %collective-permute-start.18 = (f32[16,128,128]{2,1,0:T(8,128)S(1)}, f32[16,128,128]{2,1,0:T(8,128)S(1)}, u32[]{:S(2)}, u32[]{:S(2)}) collective-permute-start(f32[16,128,128]{2,1,0:T(8,128)S(1)} %collective-permute-done.17), channel_id=1, source_target_pairs={{1,0},{2,1},{3,2},{5,4},{6,5},{7,6},{9,8},{10,9},{11,10},{13,12},{... | collective-permute-start | bytes 3145736 | tf_op jit(solution)/shard_map/ppermute | solution.py:20
  (2 other events, 4.2 us)

commit v2 on v1

--- a/solution.py
+++ b/solution.py
@@ -10,6 +10,10 @@
 
 TGX = 8
 LANES = 128
+MARK = 8
+CODE = 4096
+CHUNKS = 4
+MESH = pl.DeviceIdType.MESH
 
 step_size = 0.05
 
@@ -187,7 +191,7 @@
         intensity[...] += psi_re * psi_re + psi_im * psi_im
         return carry
 
-    lax.fori_loop(0, modes, forward, 0, unroll=2)
+    lax.fori_loop(0, modes, forward, 0, unroll=4)
 
     intensity[...] -= measured_ref[...]
     out_ref[...] = jnp.zeros_like(out_ref)
@@ -198,8 +202,8 @@
         back = inverse_transform(misfit * psi[:, :pixels], misfit * psi[:, pixels:])
         back_re, back_im = back[:, :pixels], back[:, pixels:]
         field_re, field_im = field[mode, :, :pixels], field[mode, :, pixels:]
-        out_ref[2] += field_re * back_re + field_im * back_im
-        out_ref[3] += field_re * back_im - field_im * back_re
+        out_ref[2, :pixels] += field_re * back_re + field_im * back_im
+        out_ref[3, :pixels] += field_re * back_im - field_im * back_re
         spec = forward_transform(
             patch[2] * back_re + patch[3] * back_im,
             patch[2] * back_im - patch[3] * back_re,
@@ -211,15 +215,18 @@
         )
         back_re, back_im = back[:, :pixels], back[:, pixels:]
         field_re, field_im = probe_ref[mode, 0], probe_ref[mode, 1]
-        out_ref[0] += field_re * back_re + field_im * back_im
-        out_ref[1] += field_re * back_im - field_im * back_re
+        out_ref[0, :pixels] += field_re * back_re + field_im * back_im
+        out_ref[1, :pixels] += field_re * back_im - field_im * back_re
         return carry
 
-    lax.fori_loop(0, modes, backward, 0, unroll=2)
+    lax.fori_loop(0, modes, backward, 0, unroll=4)
 
     @pl.when(live == 0)
     def _():
         out_ref[...] = jnp.zeros_like(out_ref)
+
+    code = (row * CODE + column).astype(jnp.float32)
+    out_ref[:, pixels:, :] = jnp.full((components, MARK, pixels), code)
 
 
 def position_gradient(place, tiles, halo, probe, wave, measured, matrices):
@@ -229,7 +236,7 @@
     products = 6 * modes * 2 * 2 * (2 * pixels) ** 2 * pixels
     return pl.pallas_call(
         position_kernel,
-        out_shape=jax.ShapeDtypeStruct((components, pixels, pixels), jnp.float32),
+        out_shape=jax.ShapeDtypeStruct((components, pixels + MARK, pixels), jnp.float32),
         in_specs=[scalar_spec()] + [full_spec()] * 6,
         out_specs=full_spec(),
         scratch_shapes=[
@@ -244,18 +251,19 @@
     )(place, tiles, halo, probe, wave, measured, matrices)
 
 
-def scatter_kernel(row_ref, column_ref, patch_ref, own_ref, spill_ref, canvas):
-    count, pixels = patch_ref.shape[0], patch_ref.shape[1]
+def scatter_kernel(*refs):
+    *patch_refs, own_ref, spill_ref, canvas = refs
+    pixels = patch_refs[0].shape[1]
     band_rows = own_ref.shape[1]
     canvas[...] = jnp.zeros_like(canvas)
-
-    def body(index, carry):
-        row = row_ref[index]
-        column = column_ref[index]
-        first = column // LANES
-        shift = column % LANES
-        left = pltpu.roll(patch_ref[index, :, :LANES], shift, 1)
-        right = pltpu.roll(patch_ref[index, :, LANES:], shift, 1)
+    for patch_ref in patch_refs:
+        code = jnp.max(patch_ref[pixels:, :LANES]).astype(jnp.int32)
+        row = lax.div(code, CODE)
+        column = lax.rem(code, CODE)
+        first = lax.div(column, LANES)
+        shift = lax.rem(column, LANES)
+        left = pltpu.roll(patch_ref[:pixels, :LANES], shift, 1)
+        right = pltpu.roll(patch_ref[:pixels, LANES:], shift, 1)
         lane = lax.broadcasted_iota(jnp.int32, left.shape, 1)
         late = lane >= shift
         zero = jnp.zeros_like(left)
@@ -263,24 +271,185 @@
         canvas[first, rows, :] += jnp.where(late, left, zero)
         canvas[first + 1, rows, :] += jnp.where(late, right, left)
         canvas[first + 2, rows, :] += jnp.where(late, zero, right)
-        return carry
-
-    lax.fori_loop(0, count, body, 0)
     tiles = own_ref.shape[0]
     own_ref[...] = canvas[:tiles, :band_rows, :]
     spill_ref[...] = canvas[:tiles, band_rows:, :]
 
 
-def scatter(rows, columns, patches, band_rows):
+def scatter(patches, band_rows):
     shape = jax.ShapeDtypeStruct((TGX, band_rows, LANES), jnp.float32)
     return pl.pallas_call(
         scatter_kernel,
         out_shape=(shape, shape),
-        in_specs=[scalar_spec(), scalar_spec(), full_spec()],
+        in_specs=[full_spec()] * len(patches),
         out_specs=(full_spec(), full_spec()),
         scratch_shapes=[pltpu.VMEM((TGX + 1, 2 * band_rows, LANES), jnp.float32)],
         compiler_params=pltpu.CompilerParams(vmem_limit_bytes=32 * 1024 * 1024),
-    )(rows, columns, patches)
+    )(*patches)
+
+
+def finish_kernel(
+    regions,
+    groups,
+    tiles_ref,
+    own_ref,
+    spill_ref,
+    out_ref,
+    arrived,
+    spill_send,
+    spill_recv,
+    right_send,
+    right_recv,
+    left_send,
+    left_recv,
+):
+    band = lax.axis_index("region")
+    me = lax.axis_index("pos")
+    band_tiles, across, side, _ = tiles_ref.shape
+    width = across // CHUNKS
+    above, below = band > 0, band < regions - 1
+    has_left, has_right = me > 0, me < groups - 1
+    partners = (
+        (above, {"region": band - 1}),
+        (below, {"region": band + 1}),
+        (has_left, {"pos": me - 1}),
+        (has_right, {"pos": me + 1}),
+    )
+
+    barrier = pltpu.get_barrier_semaphore()
+    for exists, where in partners:
+
+        @pl.when(exists)
+        def _():
+            pl.semaphore_signal(barrier, inc=1, device_id=where, device_id_type=MESH)
+
+    pl.semaphore_wait(barrier, sum(exists.astype(jnp.int32) for exists, _ in partners))
+
+    def columns(chunk):
+        return slice(chunk * width, (chunk + 1) * width)
+
+    def spill_copy(chunk):
+        return pltpu.make_async_remote_copy(
+            src_ref=spill_ref.at[columns(chunk)],
+            dst_ref=arrived.at[columns(chunk)],
+            send_sem=spill_send.at[chunk],
+            recv_sem=spill_recv.at[chunk],
+            device_id={"region": band + 1},
+            device_id_type=MESH,
+        )
+
+    def rightward(owner, step, chunk):
+        part = out_ref.at[:, columns(chunk), owner]
+        return pltpu.make_async_remote_copy(
+            src_ref=part,
+            dst_ref=part,
+            send_sem=right_send.at[step, chunk],
+            recv_sem=right_recv.at[step, chunk],
+            device_id={"pos": me + 1},
+            device_id_type=MESH,
+        )
+
+    def leftward(owner, step, chunk):
+        part = out_ref.at[:, columns(chunk), owner]
+        return pltpu.make_async_remote_copy(
+            src_ref=part,
+            dst_ref=part,
+            send_sem=left_send.at[step, chunk],
+            recv_sem=left_recv.at[step, chunk],
+            device_id={"pos": me - 1},
+            device_id_type=MESH,
+        )
+
+    @pl.when(below)
+    def _():
+        for chunk in range(CHUNKS):
+            spill_copy(chunk).start()
+
+    @pl.when(band == 0)
+    def _():
+        arrived[...] = jnp.zeros_like(arrived)
+
+    for chunk in range(CHUNKS):
+
+        @pl.when(above)
+        def _():
+            spill_copy(chunk).wait_recv()
+
+        for tile in range(chunk * width, (chunk + 1) * width):
+            for row in range(band_tiles):
+                lines = slice(row * side, (row + 1) * side)
+                total = own_ref[tile, lines, :] + arrived[tile, lines, :]
+                out_ref[row, tile, me] = tiles_ref[row, tile] - step_size * total
+
+        @pl.when(has_right)
+        def _():
+            rightward(me, 0, chunk).start()
+
+        @pl.when(has_left)
+        def _():
+            leftward(me, 0, chunk).start()
+
+    for step in range(1, groups):
+        for chunk in range(CHUNKS):
+
+            @pl.when(me >= step)
+            def _():
+                rightward(me - step, step - 1, chunk).wait_recv()
+
+            if step < groups - 1:
+
+                @pl.when((me >= step) & has_right)
+                def _():
+                    rightward(me - step, step, chunk).start()
+
+            @pl.when(me + step < groups)
+            def _():
+                leftward(me + step, step - 1, chunk).wait_recv()
+
+            if step < groups - 1:
+
+                @pl.when((me + step < groups) & has_left)
+                def _():
+                    leftward(me + step, step, chunk).start()
+
+    for chunk in range(CHUNKS):
+
+        @pl.when(below)
+        def _():
+            spill_copy(chunk).wait_send()
+
+        for step in range(groups - 1):
+
+            @pl.when((me >= step) & has_right)
+            def _():
+                rightward(me - step, step, chunk).wait_send()
+
+            @pl.when((me + step < groups) & has_left)
+            def _():
+                leftward(me + step, step, chunk).wait_send()
+
+
+def finish(tiles, own, spill, groups, regions):
+    band_tiles, across, side, _ = tiles.shape
+    sems = pltpu.SemaphoreType.DMA((groups - 1, CHUNKS))
+    return pl.pallas_call(
+        functools.partial(finish_kernel, regions, groups),
+        out_shape=jax.ShapeDtypeStruct((band_tiles, across, groups, side, side), jnp.float32),
+        in_specs=[full_spec()] * 3,
+        out_specs=full_spec(),
+        scratch_shapes=[
+            pltpu.VMEM(own.shape, jnp.float32),
+            pltpu.SemaphoreType.DMA((CHUNKS,)),
+            pltpu.SemaphoreType.DMA((CHUNKS,)),
+            sems,
+            sems,
+            sems,
+            sems,
+        ],
+        compiler_params=pltpu.CompilerParams(
+            collective_id=0, has_side_effects=True, vmem_limit_bytes=32 * 1024 * 1024
+        ),
+    )(tiles, own, spill)
 
 
 def dense_update(object_tiles, gradients, rows, columns, band_rows):
@@ -327,33 +496,18 @@
         for slot in range(slots)
     ]
     if groups != components:
+        gradients = [gradient[:, :pixels] for gradient in gradients]
         return dense_update(object_tiles, gradients, rows, columns, band_rows)
 
-    corner = jnp.stack([rows, columns])
-    corners = [corner] + [rotated(corner, "pos", by) for by in range(1, groups)]
     parts = []
     for gradient in gradients:
         for by in range(groups):
             piece = lax.dynamic_index_in_dim(gradient, lax.rem(me + by, groups), 0, keepdims=False)
             parts.append(piece if by == 0 else rotated(piece, "pos", by))
-    all_rows = jnp.stack([corners[by][0, slot] for slot in range(slots) for by in range(groups)])
-    all_columns = jnp.stack([corners[by][1, slot] for slot in range(slots) for by in range(groups)])
-    own, spill = scatter(all_rows, all_columns, jnp.stack(parts), band_rows)
-    arrived = shifted(spill, "region", 1)
-    total = (own + arrived).reshape(TGX, band_tiles, side, side).transpose(1, 0, 2, 3)
-    total = total.reshape(held, side, side)
-    mine = lax.dynamic_index_in_dim(tiles, me, 1, keepdims=False) - step_size * total
-
-    rightward, leftward = [mine], [mine]
-    for _ in range(groups - 1):
-        rightward.append(shifted(rightward[-1], "pos", 1))
-        leftward.append(shifted(leftward[-1], "pos", -1))
-    found = [mine] + [leftward[by] + rightward[groups - by] for by in range(1, groups)]
-    result = jnp.zeros_like(tiles)
-    for by in range(groups):
-        result = lax.dynamic_update_slice_in_dim(
-            result, found[by][:, None], lax.rem(me + by, groups), 1
-        )
+    own, spill = scatter(parts, band_rows)
+    mine = lax.dynamic_index_in_dim(tiles, me, 1, keepdims=False)
+    mine = mine.reshape(band_tiles, TGX, side, side)
+    result = finish(mine, own, spill, groups, lax.axis_size("region"))
     return result.reshape(object_tiles.shape)
 
 

time: 213 us -> 173 us (0.81)
  waiting for transfers between devices: 103 us -> 31.7 us
  Pallas kernels: 40.8 us -> 111 us
  starting transfers between devices: 39.3 us -> 16.4 us
  local copies, waits for them, and re-layouts: 22.3 us -> 8.74 us
    ppermute x10 -> x3, waiting for transfers between devices: 85.7 us -> 8.85 us  [shifted(): return lax.ppermute(shard, axis, pairs)]
    pallas_call x1 -> x2, Pallas kernels: 2.89 us -> 75.7 us  [the longest x1 73.9 us: finish(): pl.pallas_call(functools.partial(finish_kernel, regions, groups), out_sha...]
    ppermute x10 -> x3, starting transfers between devices: 24.9 us -> 7.77 us  [shifted(): return lax.ppermute(shard, axis, pairs)]
    another operation x3 -> x0, local copies, waits for them, and re-layouts: 10 us -> none  [the longest x1 5.03 us: per_device(): jnp.stack([corners[by][1, slot] for slot in range(slots) for by in range(...]
    ppermute x9 -> x6, starting transfers between devices: 14.4 us -> 8.62 us  [rotated(): lax.ppermute(shard, axis, [(i, (i + by) % count) for i in range(count)])]
    ppermute x9 -> x6, waiting for transfers between devices: 17.6 us -> 22.9 us  [rotated(): lax.ppermute(shard, axis, [(i, (i + by) % count) for i in range(count)])]
    slice x5 -> x0, local copies, waits for them, and re-layouts: 2.99 us -> none  [the longest x4 2.35 us: per_device(): corners[by][1, slot]]
    pallas_call x2, Pallas kernels: 36 us -> 33.8 us  [position_gradient(): pl.pallas_call(position_kernel, out_shape=jax.ShapeDtypeStruct((component...]
  transfers between devices with their start and end apart: 19 -> 9, of which waited for: 9 -> 3; matrix products, arithmetic and copies ran while one was open for 9% -> 4% of each run, Pallas kernels for 18% -> 20%
where the time goes in v2:
time: 173 us; the launch traced here: 172 us
  Pallas kernels  111 us (64%)
  waiting for transfers between devices  31.7 us (18%)
  starting transfers between devices  16.4 us (9%)
  local copies, waits for them, and re-layouts  8.74 us (5%)
  other arithmetic  2.99 us (2%)
    pallas_call x1, Pallas kernels, finish(): pl.pallas_call(functools.partial(finish_kernel, regions, groups), out_sha...  73.9 us
    pallas_call x2, Pallas kernels, position_gradient(): pl.pallas_call(position_kernel, out_shape=jax.ShapeDtypeStruct((component...  33.8 us
    ppermute x6, waiting for transfers between devices, rotated(): lax.ppermute(shard, axis, [(i, (i + by) % count) for i in range(count)])  22.9 us
    ppermute x3, waiting for transfers between devices, shifted(): return lax.ppermute(shard, axis, pairs)  8.85 us
    ppermute x6, starting transfers between devices, rotated(): lax.ppermute(shard, axis, [(i, (i + by) % count) for i in range(count)])  8.62 us
    ppermute x3, starting transfers between devices, shifted(): return lax.ppermute(shard, axis, pairs)  7.77 us
    unnamed x11, local copies, waits for them, and re-layouts  4.23 us
  transfers between devices with their start and end apart: 9, of which 3 were waited for; matrix products, arithmetic and copies ran while one was open for 4% of the time, Pallas kernels for 20%

profile of v2, /device:TPU:2, one launch (start us, length us, event | category | flops | bytes accessed | tf_op | source)
XLA Modules:
  0.0 172.1 jit_solution(13936190649335031501)
XLA Ops:
  0.0 1.9 %collective-permute-start = (s32[2]{0:T(128)}, s32[2]{0:T(128)S(1)}, u32[]{:S(2)}, u32[]{:S(2)}) collective-permute-start(s32[2]{0:T(128)} %bitcast.47), channel_id=1, source_target_pairs={{0,4},{4,8},{8,12},{12,16},{16,20},{20,24},{24,28},{1,5},{5,9},{9,... | collective-permute-start | bytes 32 | tf_op jit(solution)/shard_map/ppermute | solution.py:24
  1.9 1.0 fusion.10
  2.9 1.1 multiply_convert_fusion
  4.7 0.7 subtract_bitcast_fusion
  5.4 2.2 %copy-done = f32[16,2,2,128,128]{4,3,2,1,0:T(8,128)S(1)} copy-done((f32[16,2,2,128,128]{4,3,2,1,0:T(8,128)S(1)}, f32[16,2,2,128,128]{4,3,2,1,0:T(8,128)}, u32[]{:S(2)}) %copy-start) | copy-done | bytes 4194328
  7.6 1.9 %shard_map.73 = f32[2,4,256,256]{3,2,1,0:T(8,128)S(1)} custom-call(s32[2]{0:T(128)S(1)} %collective-permute-done.column_ref, f32[16,4,128,128]{3,2,1,0:T(8,128)S(1)} %bitcast.45), custom_call_target="tpu_custom_call" | custom-call | tf_op jit(solution)/shard_map/pallas_call | solution.py:108
  9.5 1.1 slice_bitcast_fusion
  10.6 3.6 %collective-permute-start.5 = (f32[4,256,256]{2,1,0:T(8,128)}, f32[4,256,256]{2,1,0:T(8,128)S(1)}, u32[]{:S(2)}, u32[]{:S(2)}) collective-permute-start(f32[4,256,256]{2,1,0:T(8,128)} %get-tuple-element.11), channel_id=1, source_target_pairs={{4,0},{8,4},{12,8},{16,12},{20,16},{24,20},{28,24},{5,1},{9,5},{13... | collective-permute-start | bytes 3145736 | tf_op jit(solution)/shard_map/ppermute | solution.py:24
  14.3 1.0 cosine_bitcast_fusion
  15.6 2.2 %collective-permute-start.1 = (f32[4,256,256]{2,1,0:T(8,128)S(1)}, f32[4,256,256]{2,1,0:T(8,128)S(1)}, u32[]{:S(2)}, u32[]{:S(2)}) collective-permute-start(f32[4,256,256]{2,1,0:T(8,128)S(1)} %get-tuple-element.12), channel_id=1, source_target_pairs={{4,0},{8,4},{12,8},{16,12},{20,16},{24,20},{28,24},{5,1},{9,5},{13... | collective-permute-start | bytes 3145736 | tf_op jit(solution)/shard_map/ppermute | solution.py:24
  18.0 8.8 %collective-permute-done.5.halo_ref = f32[4,256,256]{2,1,0:T(8,128)S(1)} collective-permute-done((f32[4,256,256]{2,1,0:T(8,128)}, f32[4,256,256]{2,1,0:T(8,128)S(1)}, u32[]{:S(2)}, u32[]{:S(2)}) %collective-permute-start.5) | collective-permute-done | bytes 1048608 | tf_op jit(solution)/shard_map/ppermute | solution.py:24
  26.9 16.9 %shard_map.75 = f32[4,264,256]{2,1,0:T(8,128)S(1)} custom-call(s32[3]{0:T(128)S(1)} %get-tuple-element.9.place_ref, f32[16,4,128,128]{3,2,1,0:T(8,128)} %bitcast.42, f32[4,256,256]{2,1,0:T(8,128)S(1)} %collective-permute-done.5.halo_ref, f32[4,2,256,256]{3,2,1,0:T(8,128)S(1)} %copy-done.1, f32[2,256,256]{2,1,0:T(8,128)S(1)} %pad_maximum_fusion.5.wave_ref, ...), custom_call_target="tpu_custom_call" | custom-call | flops 6442450944 | bytes 12582912 | tf_op jit(solution)/shard_map/pallas_call | solution.py:237
  43.9 3.7 %collective-permute-start.8 = (f32[264,256]{1,0:T(8,128)S(1)}, f32[264,256]{1,0:T(8,128)S(1)}, u32[]{:S(2)}, u32[]{:S(2)}) collective-permute-start(f32[264,256]{1,0:T(8,128)S(1)} %get-tuple-element.13), channel_id=1, source_target_pairs={{0,3},{1,0},{2,1},{3,2},{4,7},{5,4},{6,5},{7,6},{8,11},{9,8},{10,9... | collective-permute-start | bytes 811016 | tf_op jit(solution)/shard_map/ppermute | solution.py:29
  47.6 1.0 collective-permute-start.6
  48.6 16.9 %shard_map.74 = f32[4,264,256]{2,1,0:T(8,128)S(1)} custom-call(s32[3]{0:T(128)S(1)} %get-tuple-element.10.place_ref, f32[16,4,128,128]{3,2,1,0:T(8,128)} %bitcast.43, f32[4,256,256]{2,1,0:T(8,128)S(1)} %collective-permute-done.1.halo_ref, f32[4,2,256,256]{3,2,1,0:T(8,128)S(1)} %copy-done.1, f32[2,256,256]{2,1,0:T(8,128)S(1)} %pad_maximum_fusion.5.wave_ref, ...), custom_call_target="tpu_custom_call" | custom-call | flops 6442450944 | bytes 12582912 | tf_op jit(solution)/shard_map/pallas_call | solution.py:237
  65.5 0.8 dynamic-slice_bitcast_fusion.4
  66.3 2.8 %collective-permute-start.4 = (f32[264,256]{1,0:T(8,128)}, f32[264,256]{1,0:T(8,128)S(1)}, u32[]{:S(2)}, u32[]{:S(2)}) collective-permute-start(f32[264,256]{1,0:T(8,128)} %get-tuple-element.17), channel_id=1, source_target_pairs={{0,3},{1,0},{2,1},{3,2},{4,7},{5,4},{6,5},{7,6},{8,11},{9,8},{10,9... | collective-permute-start | bytes 811016 | tf_op jit(solution)/shard_map/ppermute | solution.py:29
  69.1 1.1 collective-permute-start.3
  70.2 1.3 constant_dynamic-slice_fusion
  71.6 5.8 %collective-permute-done.4.refs_3_ = f32[264,256]{1,0:T(8,128)S(1)} collective-permute-done((f32[264,256]{1,0:T(8,128)}, f32[264,256]{1,0:T(8,128)S(1)}, u32[]{:S(2)}, u32[]{:S(2)}) %collective-permute-start.4) | collective-permute-done | bytes 270368 | tf_op jit(solution)/shard_map/ppermute | solution.py:29
  77.4 17.0 %collective-permute-done.3.refs_2_ = f32[264,256]{1,0:T(8,128)S(1)} collective-permute-done((f32[264,256]{1,0:T(8,128)S(1)}, f32[264,256]{1,0:T(8,128)S(1)}, u32[]{:S(2)}, u32[]{:S(2)}) %collective-permute-start.3) | collective-permute-done | bytes 270368 | tf_op jit(solution)/shard_map/ppermute | solution.py:29
  94.4 1.7 %shard_map.76 = (f32[8,256,128]{2,1,0:T(8,128)S(1)}, f32[8,256,128]{2,1,0:T(8,128)S(1)}) custom-call(f32[264,256]{1,0:T(8,128)S(1)} %get-tuple-element.20.refs_0_, f32[264,256]{1,0:T(8,128)S(1)} %collective-permute-done.2.refs_1_, f32[264,256]{1,0:T(8,128)S(1)} %collective-permute-done.3.refs_2_, f32[264,256]{1,0:T(8,128)S(1)} %collective-permute-done.4.refs_3_, ...), custom_call_target="tpu_custom_call" | custom-call | tf_op jit(solution)/shard_map/pallas_call | solution.py:281
  96.2 73.9 %shard_map.77 = f32[2,8,4,128,128]{4,3,2,1,0:T(8,128)S(1)} custom-call(f32[2,8,128,128]{3,2,1,0:T(8,128)S(1)} %bitcast.46, f32[8,256,128]{2,1,0:T(8,128)S(1)} %get-tuple-element.7.own_ref, f32[8,256,128]{2,1,0:T(8,128)S(1)} %get-tuple-element.8.spill_ref), custom_call_target="tpu_custom_call" | custom-call | tf_op jit(solution)/shard_map/pallas_call | solution.py:435
  170.1 2.0 %copy.10 = f32[16,2,2,128,128]{4,3,2,1,0:T(8,128)} copy(f32[16,2,2,128,128]{4,3,2,1,0:T(8,128)S(1)} %bitcast.41) | data formatting | bytes 8388608
  (25 shorter events, 0.6 us)
Async XLA Ops:
  0.0 5.4 %collective-permute-start = (s32[2]{0:T(128)}, s32[2]{0:T(128)S(1)}, u32[]{:S(2)}, u32[]{:S(2)}) collective-permute-start(s32[2]{0:T(128)} %bitcast.47), channel_id=1, source_target_pairs={{0,4},{4,8},{8,12},{12,16},{16,20},{20,24},{24,28},{1,5},{5,9},{9,... | collective-permute-start | bytes 32 | tf_op jit(solution)/shard_map/ppermute | solution.py:24
  5.4 2.2 %copy-start = (f32[16,2,2,128,128]{4,3,2,1,0:T(8,128)S(1)}, f32[16,2,2,128,128]{4,3,2,1,0:T(8,128)}, u32[]{:S(2)}) copy-start(f32[16,2,2,128,128]{4,3,2,1,0:T(8,128)} %param.7) | copy-start | bytes 12582916
  9.5 4.8 %copy-start.4 = (s32[1,1,2]{2,1,0:T(1,128)S(1)}, s32[1,1,2]{2,1,0:T(1,128)}, u32[]{:S(2)}) copy-start(s32[1,1,2]{2,1,0:T(1,128)} %param.12) | copy-start | bytes 28
  9.5 4.8 %copy-start.3 = (f32[256,256]{1,0:T(8,128)S(1)}, f32[256,256]{1,0:T(8,128)}, u32[]{:S(2)}) copy-start(f32[256,256]{1,0:T(8,128)} %param.9) | copy-start | bytes 786436
  10.6 16.2 %collective-permute-start.5 = (f32[4,256,256]{2,1,0:T(8,128)}, f32[4,256,256]{2,1,0:T(8,128)S(1)}, u32[]{:S(2)}, u32[]{:S(2)}) collective-permute-start(f32[4,256,256]{2,1,0:T(8,128)} %get-tuple-element.11), channel_id=1, source_target_pairs={{4,0},{8,4},{12,8},{16,12},{20,16},{24,20},{28,24},{5,1},{9,5},{13... | collective-permute-start | bytes 3145736 | tf_op jit(solution)/shard_map/ppermute | solution.py:24
  15.3 2.7 %copy-start.2 = (f32[1,1,2,256,256]{4,3,2,1,0:T(8,128)S(1)}, f32[1,1,2,256,256]{4,3,2,1,0:T(8,128)}, u32[]{:S(2)}) copy-start(f32[1,1,2,256,256]{4,3,2,1,0:T(8,128)} %param.10) | copy-start | bytes 1572868
  15.4 11.5 %copy-start.1 = (f32[4,2,256,256]{3,2,1,0:T(8,128)S(1)}, f32[4,2,256,256]{3,2,1,0:T(8,128)}, u32[]{:S(2)}) copy-start(f32[4,2,256,256]{3,2,1,0:T(8,128)} %probe_ref.3) | copy-start | bytes 6291460
  15.6 33.0 %collective-permute-start.1 = (f32[4,256,256]{2,1,0:T(8,128)S(1)}, f32[4,256,256]{2,1,0:T(8,128)S(1)}, u32[]{:S(2)}, u32[]{:S(2)}) collective-permute-start(f32[4,256,256]{2,1,0:T(8,128)S(1)} %get-tuple-element.12), channel_id=1, source_target_pairs={{4,0},{8,4},{12,8},{16,12},{20,16},{24,20},{28,24},{5,1},{9,5},{13... | collective-permute-start | bytes 3145736 | tf_op jit(solution)/shard_map/ppermute | solution.py:24
  43.9 26.3 %collective-permute-start.8 = (f32[264,256]{1,0:T(8,128)S(1)}, f32[264,256]{1,0:T(8,128)S(1)}, u32[]{:S(2)}, u32[]{:S(2)}) collective-permute-start(f32[264,256]{1,0:T(8,128)S(1)} %get-tuple-element.13), channel_id=1, source_target_pairs={{0,3},{1,0},{2,1},{3,2},{4,7},{5,4},{6,5},{7,6},{8,11},{9,8},{10,9... | collective-permute-start | bytes 811016 | tf_op jit(solution)/shard_map/ppermute | solution.py:29
  47.6 24.0 %collective-permute-start.7 = (f32[264,256]{1,0:T(8,128)S(1)}, f32[264,256]{1,0:T(8,128)S(1)}, u32[]{:S(2)}, u32[]{:S(2)}) collective-permute-start(f32[264,256]{1,0:T(8,128)S(1)} %get-tuple-element.14), channel_id=1, source_target_pairs={{0,2},{1,3},{2,0},{3,1},{4,6},{5,7},{6,4},{7,5},{8,10},{9,11},{10,... | collective-permute-start | bytes 811016 | tf_op jit(solution)/shard_map/ppermute | solution.py:29
  47.6 24.0 %collective-permute-start.6 = (f32[264,256]{1,0:T(8,128)S(1)}, f32[264,256]{1,0:T(8,128)S(1)}, u32[]{:S(2)}, u32[]{:S(2)}) collective-permute-start(f32[264,256]{1,0:T(8,128)S(1)} %get-tuple-element.15), channel_id=1, source_target_pairs={{0,1},{1,2},{2,3},{3,0},{4,5},{5,6},{6,7},{7,4},{8,9},{9,10},{10,1... | collective-permute-start | bytes 811016 | tf_op jit(solution)/shard_map/ppermute | solution.py:29
  66.3 11.1 %collective-permute-start.4 = (f32[264,256]{1,0:T(8,128)}, f32[264,256]{1,0:T(8,128)S(1)}, u32[]{:S(2)}, u32[]{:S(2)}) collective-permute-start(f32[264,256]{1,0:T(8,128)} %get-tuple-element.17), channel_id=1, source_target_pairs={{0,3},{1,0},{2,1},{3,2},{4,7},{5,4},{6,5},{7,6},{8,11},{9,8},{10,9... | collective-permute-start | bytes 811016 | tf_op jit(solution)/shard_map/ppermute | solution.py:29
  69.1 25.3 %collective-permute-start.3 = (f32[264,256]{1,0:T(8,128)S(1)}, f32[264,256]{1,0:T(8,128)S(1)}, u32[]{:S(2)}, u32[]{:S(2)}) collective-permute-start(f32[264,256]{1,0:T(8,128)S(1)} %get-tuple-element.18), channel_id=1, source_target_pairs={{0,2},{1,3},{2,0},{3,1},{4,6},{5,7},{6,4},{7,5},{8,10},{9,11},{10,... | collective-permute-start | bytes 811016 | tf_op jit(solution)/shard_map/ppermute | solution.py:29
  70.2 24.2 %collective-permute-start.2 = (f32[264,256]{1,0:T(8,128)S(1)}, f32[264,256]{1,0:T(8,128)S(1)}, u32[]{:S(2)}, u32[]{:S(2)}) collective-permute-start(f32[264,256]{1,0:T(8,128)S(1)} %get-tuple-element.19), channel_id=1, source_target_pairs={{0,1},{1,2},{2,3},{3,0},{4,5},{5,6},{6,7},{7,4},{8,9},{9,10},{10,1... | collective-permute-start | bytes 811016 | tf_op jit(solution)/shard_map/ppermute | solution.py:29

commit v3 on v2

--- a/solution.py
+++ b/solution.py
@@ -128,6 +128,8 @@
     field,
     far,
     intensity,
+    stacked,
+    middle,
 ):
     row = place_ref[0]
     column = place_ref[1]
@@ -154,72 +156,75 @@
 
     lax.fori_loop(0, components, fill, 0)
 
-    def transform(real, imag, left, right):
-        stacked = jnp.concatenate([real, imag], axis=0).astype(jnp.bfloat16)
-        upper = jnp.dot(matrix_ref[left], stacked, preferred_element_type=jnp.float32)
-        upper = upper.astype(jnp.bfloat16)
-        upper = jnp.concatenate([upper[:pixels], upper[pixels:]], axis=1)
-        return jnp.dot(upper, matrix_ref[right], preferred_element_type=jnp.float32)
-
-    def forward_transform(real, imag):
-        return transform(real, imag, minus, plus)
-
-    def inverse_transform(real, imag):
-        return transform(real, imag, plus, minus)
-
-    intensity[...] = jnp.zeros_like(intensity)
-
-    def forward(mode, carry):
-        field_re, field_im = probe_ref[mode, 0], probe_ref[mode, 1]
-        spec = forward_transform(
-            field_re * patch[0] - field_im * patch[1],
-            field_re * patch[1] + field_im * patch[0],
-        )
-        spec_re, spec_im = spec[:, :pixels], spec[:, pixels:]
-        moved = inverse_transform(
-            wave_ref[0] * spec_re - wave_ref[1] * spec_im,
-            wave_ref[0] * spec_im + wave_ref[1] * spec_re,
-        )
-        field[mode] = moved
-        field_re, field_im = moved[:, :pixels], moved[:, pixels:]
-        psi = forward_transform(
-            field_re * patch[2] - field_im * patch[3],
-            field_re * patch[3] + field_im * patch[2],
-        )
-        far[mode] = psi
-        psi_re, psi_im = psi[:, :pixels], psi[:, pixels:]
-        intensity[...] += psi_re * psi_re + psi_im * psi_im
-        return carry
-
-    lax.fori_loop(0, modes, forward, 0, unroll=4)
-
-    intensity[...] -= measured_ref[...]
-    out_ref[...] = jnp.zeros_like(out_ref)
-
-    def backward(mode, carry):
-        misfit = intensity[...]
-        psi = far[mode]
-        back = inverse_transform(misfit * psi[:, :pixels], misfit * psi[:, pixels:])
-        back_re, back_im = back[:, :pixels], back[:, pixels:]
-        field_re, field_im = field[mode, :, :pixels], field[mode, :, pixels:]
-        out_ref[2, :pixels] += field_re * back_re + field_im * back_im
-        out_ref[3, :pixels] += field_re * back_im - field_im * back_re
-        spec = forward_transform(
-            patch[2] * back_re + patch[3] * back_im,
-            patch[2] * back_im - patch[3] * back_re,
-        )
-        spec_re, spec_im = spec[:, :pixels], spec[:, pixels:]
-        back = inverse_transform(
-            wave_ref[0] * spec_re + wave_ref[1] * spec_im,
-            wave_ref[0] * spec_im - wave_ref[1] * spec_re,
-        )
-        back_re, back_im = back[:, :pixels], back[:, pixels:]
-        field_re, field_im = probe_ref[mode, 0], probe_ref[mode, 1]
-        out_ref[0, :pixels] += field_re * back_re + field_im * back_im
-        out_ref[1, :pixels] += field_re * back_im - field_im * back_re
-        return carry
-
-    lax.fori_loop(0, modes, backward, 0, unroll=4)
+    def transform(left, right):
+        upper = jnp.dot(matrix_ref[left], stacked[...], preferred_element_type=jnp.float32)
+        for mode in range(modes):
+            lines = slice(mode * pixels, (mode + 1) * pixels)
+            middle[lines, :pixels] = upper[:pixels, lines].astype(jnp.bfloat16)
+            middle[lines, pixels:] = upper[pixels:, lines].astype(jnp.bfloat16)
+        return jnp.dot(middle[...], matrix_ref[right], preferred_element_type=jnp.float32)
+
+    def forward_transform():
+        return transform(minus, plus)
+
+    def inverse_transform():
+        return transform(plus, minus)
+
+    def put(mode, real, imag):
+        lanes = slice(mode * pixels, (mode + 1) * pixels)
+        stacked[:pixels, lanes] = real.astype(jnp.bfloat16)
+        stacked[pixels:, lanes] = imag.astype(jnp.bfloat16)
+
+    def pick(value, mode):
+        lines = value[mode * pixels : (mode + 1) * pixels]
+        return lines[:, :pixels], lines[:, pixels:]
+
+    for mode in range(modes):
+        u_re, u_im = probe_ref[mode, 0], probe_ref[mode, 1]
+        put(mode, u_re * patch[0] - u_im * patch[1], u_re * patch[1] + u_im * patch[0])
+    spec = forward_transform()
+    for mode in range(modes):
+        re, im = pick(spec, mode)
+        put(mode, wave_ref[0] * re - wave_ref[1] * im, wave_ref[0] * im + wave_ref[1] * re)
+    moved = inverse_transform()
+    for mode in range(modes):
+        u_re, u_im = pick(moved, mode)
+        field[mode, :, :pixels] = u_re
+        field[mode, :, pixels:] = u_im
+        put(mode, u_re * patch[2] - u_im * patch[3], u_re * patch[3] + u_im * patch[2])
+    psi = forward_transform()
+    total = -measured_ref[...]
+    for mode in range(modes):
+        re, im = pick(psi, mode)
+        far[mode, :, :pixels] = re
+        far[mode, :, pixels:] = im
+        total += re * re + im * im
+    intensity[...] = total
+    for mode in range(modes):
+        put(mode, intensity[...] * far[mode, :, :pixels], intensity[...] * far[mode, :, pixels:])
+    back = inverse_transform()
+    grad_re, grad_im = 0.0, 0.0
+    for mode in range(modes):
+        b_re, b_im = pick(back, mode)
+        u_re, u_im = field[mode, :, :pixels], field[mode, :, pixels:]
+        grad_re += u_re * b_re + u_im * b_im
+        grad_im += u_re * b_im - u_im * b_re
+        put(mode, patch[2] * b_re + patch[3] * b_im, patch[2] * b_im - patch[3] * b_re)
+    out_ref[2, :pixels] = grad_re
+    out_ref[3, :pixels] = grad_im
+    spec = forward_transform()
+    for mode in range(modes):
+        re, im = pick(spec, mode)
+        put(mode, wave_ref[0] * re + wave_ref[1] * im, wave_ref[0] * im - wave_ref[1] * re)
+    back = inverse_transform()
+    grad_re, grad_im = 0.0, 0.0
+    for mode in range(modes):
+        b_re, b_im = pick(back, mode)
+        u_re, u_im = probe_ref[mode, 0], probe_ref[mode, 1]
+        grad_re += u_re * b_re + u_im * b_im
+        grad_im += u_re * b_im - u_im * b_re
+    out_ref[0, :pixels] = grad_re
+    out_ref[1, :pixels] = grad_im
 
     @pl.when(live == 0)
     def _():
@@ -245,6 +250,8 @@
             pltpu.VMEM((modes, pixels, 2 * pixels), jnp.float32),
             pltpu.VMEM((modes, pixels, 2 * pixels), jnp.float32),
             pltpu.VMEM((pixels, pixels), jnp.float32),
+            pltpu.VMEM((2 * pixels, modes * pixels), jnp.bfloat16),
+            pltpu.VMEM((modes * pixels, 2 * pixels), jnp.bfloat16),
         ],
         cost_estimate=pl.CostEstimate(flops=products, bytes_accessed=12 * 2**20, transcendentals=0),
         compiler_params=pltpu.CompilerParams(vmem_limit_bytes=48 * 1024 * 1024),
@@ -485,7 +492,12 @@
 
     wanted = shifted(columns, "region", 1)
     windows = column_windows(wanted, tiles, pixels)
-    halos = [shifted(windows[slot], "region", -1) for slot in range(slots)]
+    halos = []
+    for slot in range(slots):
+        window = windows[slot]
+        if halos:
+            window, halos[-1] = lax.optimization_barrier((window, halos[-1]))
+        halos.append(shifted(window, "region", -1))
 
     matrices = make_matrices(pixels)
     wave = jnp.stack([jnp.cos(fresnel_phase), jnp.sin(fresnel_phase)])

time: 173 us -> 168 us (0.971)
  Pallas kernels: 111 us -> 98.7 us
  waiting for transfers between devices: 31.7 us -> 40.3 us
    pallas_call x2, Pallas kernels: 33.8 us -> 21.3 us  [position_gradient(): pl.pallas_call(position_kernel, out_shape=jax.ShapeDtypeStruct((component...]
    ppermute x6, waiting for transfers between devices: 22.9 us -> 29.4 us  [rotated(): lax.ppermute(shard, axis, [(i, (i + by) % count) for i in range(count)])]
    ppermute x3, waiting for transfers between devices: 8.85 us -> 10.9 us  [shifted(): return lax.ppermute(shard, axis, pairs)]
  transfers between devices with their start and end apart: 9 -> 9, of which waited for: 3 -> 5; matrix products, arithmetic and copies ran while one was open for 4% -> 4% of each run, Pallas kernels for 20% -> 13%
where the time goes in v3:
time: 168 us
  Pallas kernels  98.7 us (59%)
  waiting for transfers between devices  40.3 us (24%)
  starting transfers between devices  16.1 us (10%)
  local copies, waits for them, and re-layouts  8.74 us (5%)
  other arithmetic  2.98 us (2%)
    pallas_call x1, Pallas kernels, finish(): pl.pallas_call(functools.partial(finish_kernel, regions, groups), out_sha...  73.7 us
    ppermute x6, waiting for transfers between devices, rotated(): lax.ppermute(shard, axis, [(i, (i + by) % count) for i in range(count)])  29.4 us
    pallas_call x2, Pallas kernels, position_gradient(): pl.pallas_call(position_kernel, out_shape=jax.ShapeDtypeStruct((component...  21.3 us
    ppermute x3, waiting for transfers between devices, shifted(): return lax.ppermute(shard, axis, pairs)  10.9 us
    ppermute x6, starting transfers between devices, rotated(): lax.ppermute(shard, axis, [(i, (i + by) % count) for i in range(count)])  8.63 us
    ppermute x3, starting transfers between devices, shifted(): return lax.ppermute(shard, axis, pairs)  7.52 us
    unnamed x11, local copies, waits for them, and re-layouts  4.23 us
  transfers between devices with their start and end apart: 9, of which 5 were waited for; matrix products, arithmetic and copies ran while one was open for 4% of the time, Pallas kernels for 13%

profile of v3, /device:TPU:2, one launch (start us, length us, event | category | flops | bytes accessed | tf_op | source)
XLA Modules:
  0.0 167.8 jit_solution(7478605881594557813)
XLA Ops:
  0.0 1.9 %collective-permute-start = (s32[2]{0:T(128)}, s32[2]{0:T(128)S(1)}, u32[]{:S(2)}, u32[]{:S(2)}) collective-permute-start(s32[2]{0:T(128)} %bitcast.47), channel_id=1, source_target_pairs={{0,4},{4,8},{8,12},{12,16},{16,20},{20,24},{24,28},{1,5},{5,9},{9,... | collective-permute-start | bytes 32 | tf_op jit(solution)/shard_map/ppermute | solution.py:24
  3.2 1.8 %collective-permute-done.column_ref = s32[2]{0:T(128)S(1)} collective-permute-done((s32[2]{0:T(128)}, s32[2]{0:T(128)S(1)}, u32[]{:S(2)}, u32[]{:S(2)}) %collective-permute-start) | collective-permute-done | bytes 40 | tf_op jit(solution)/shard_map/ppermute | solution.py:24
  5.0 2.2 %copy-done = f32[16,2,2,128,128]{4,3,2,1,0:T(8,128)S(1)} copy-done((f32[16,2,2,128,128]{4,3,2,1,0:T(8,128)S(1)}, f32[16,2,2,128,128]{4,3,2,1,0:T(8,128)}, u32[]{:S(2)}) %copy-start) | copy-done | bytes 4194328
  7.2 1.9 %shard_map.73 = f32[2,4,256,256]{3,2,1,0:T(8,128)S(1)} custom-call(s32[2]{0:T(128)S(1)} %collective-permute-done.column_ref, f32[16,4,128,128]{3,2,1,0:T(8,128)S(1)} %bitcast.45), custom_call_target="tpu_custom_call" | custom-call | tf_op jit(solution)/shard_map/pallas_call | solution.py:108
  9.1 1.1 slice_bitcast_fusion
  10.3 1.9 %collective-permute-start.1 = (f32[4,256,256]{2,1,0:T(8,128)}, f32[4,256,256]{2,1,0:T(8,128)S(1)}, u32[]{:S(2)}, u32[]{:S(2)}) collective-permute-start(f32[4,256,256]{2,1,0:T(8,128)} %get-tuple-element.15), channel_id=1, source_target_pairs={{4,0},{8,4},{12,8},{16,12},{20,16},{24,20},{28,24},{5,1},{9,5},{13... | collective-permute-start | bytes 3145736 | tf_op jit(solution)/shard_map/ppermute | solution.py:24
  12.2 1.0 fusion.10
  13.2 1.1 multiply_convert_fusion
  14.4 1.0 cosine_bitcast_fusion
  15.6 9.2 %collective-permute-done.1.halo_ref = f32[4,256,256]{2,1,0:T(8,128)S(1)} collective-permute-done((f32[4,256,256]{2,1,0:T(8,128)}, f32[4,256,256]{2,1,0:T(8,128)S(1)}, u32[]{:S(2)}, u32[]{:S(2)}) %collective-permute-start.1) | collective-permute-done | bytes 1048608 | tf_op jit(solution)/shard_map/ppermute | solution.py:24
  24.8 3.7 %collective-permute-start.5 = (f32[4,256,256]{2,1,0:T(8,128)S(1)}, f32[4,256,256]{2,1,0:T(8,128)S(1)}, u32[]{:S(2)}, u32[]{:S(2)}) collective-permute-start(f32[4,256,256]{2,1,0:T(8,128)S(1)} %get-tuple-element.10), channel_id=1, source_target_pairs={{4,0},{8,4},{12,8},{16,12},{20,16},{24,20},{28,24},{5,1},{9,5},{13... | collective-permute-start | bytes 3145736 | tf_op jit(solution)/shard_map/ppermute | solution.py:24
  28.7 10.6 %shard_map.74 = f32[4,264,256]{2,1,0:T(8,128)S(1)} custom-call(s32[3]{0:T(128)S(1)} %get-tuple-element.14.place_ref, f32[16,4,128,128]{3,2,1,0:T(8,128)} %bitcast.42, f32[4,256,256]{2,1,0:T(8,128)S(1)} %collective-permute-done.1.halo_ref, f32[4,2,256,256]{3,2,1,0:T(8,128)S(1)} %copy-done.1, f32[2,256,256]{2,1,0:T(8,128)S(1)} %pad_maximum_fusion.5.wave_ref, ...), custom_call_target="tpu_custom_call" | custom-call | flops 6442450944 | bytes 12582912 | tf_op jit(solution)/shard_map/pallas_call | solution.py:242
  39.5 3.7 %collective-permute-start.4 = (f32[264,256]{1,0:T(8,128)S(1)}, f32[264,256]{1,0:T(8,128)S(1)}, u32[]{:S(2)}, u32[]{:S(2)}) collective-permute-start(f32[264,256]{1,0:T(8,128)S(1)} %get-tuple-element.21), channel_id=1, source_target_pairs={{0,3},{1,0},{2,1},{3,2},{4,7},{5,4},{6,5},{7,6},{8,11},{9,8},{10,9... | collective-permute-start | bytes 811016 | tf_op jit(solution)/shard_map/ppermute | solution.py:29
  43.1 1.0 collective-permute-start.2
  44.1 10.7 %shard_map.75 = f32[4,264,256]{2,1,0:T(8,128)S(1)} custom-call(s32[3]{0:T(128)S(1)} %get-tuple-element.13.place_ref, f32[16,4,128,128]{3,2,1,0:T(8,128)} %bitcast.43, f32[4,256,256]{2,1,0:T(8,128)S(1)} %collective-permute-done.5.halo_ref, f32[4,2,256,256]{3,2,1,0:T(8,128)S(1)} %copy-done.1, f32[2,256,256]{2,1,0:T(8,128)S(1)} %pad_maximum_fusion.5.wave_ref, ...), custom_call_target="tpu_custom_call" | custom-call | flops 6442450944 | bytes 12582912 | tf_op jit(solution)/shard_map/pallas_call | solution.py:242
  55.6 2.8 %collective-permute-start.8 = (f32[264,256]{1,0:T(8,128)}, f32[264,256]{1,0:T(8,128)S(1)}, u32[]{:S(2)}, u32[]{:S(2)}) collective-permute-start(f32[264,256]{1,0:T(8,128)} %get-tuple-element.17), channel_id=1, source_target_pairs={{0,3},{1,0},{2,1},{3,2},{4,7},{5,4},{6,5},{7,6},{8,11},{9,8},{10,9... | collective-permute-start | bytes 811016 | tf_op jit(solution)/shard_map/ppermute | solution.py:29
  58.4 1.2 collective-permute-start.7
  59.6 1.3 constant_dynamic-slice_fusion
  60.9 6.4 %collective-permute-done.3.refs_2_ = f32[264,256]{1,0:T(8,128)S(1)} collective-permute-done((f32[264,256]{1,0:T(8,128)S(1)}, f32[264,256]{1,0:T(8,128)S(1)}, u32[]{:S(2)}, u32[]{:S(2)}) %collective-permute-start.3) | collective-permute-done | bytes 270368 | tf_op jit(solution)/shard_map/ppermute | solution.py:29
  67.3 5.6 %collective-permute-done.8.refs_7_ = f32[264,256]{1,0:T(8,128)S(1)} collective-permute-done((f32[264,256]{1,0:T(8,128)}, f32[264,256]{1,0:T(8,128)S(1)}, u32[]{:S(2)}, u32[]{:S(2)}) %collective-permute-start.8) | collective-permute-done | bytes 270368 | tf_op jit(solution)/shard_map/ppermute | solution.py:29
  72.8 17.4 %collective-permute-done.7.refs_6_ = f32[264,256]{1,0:T(8,128)S(1)} collective-permute-done((f32[264,256]{1,0:T(8,128)S(1)}, f32[264,256]{1,0:T(8,128)S(1)}, u32[]{:S(2)}, u32[]{:S(2)}) %collective-permute-start.7) | collective-permute-done | bytes 270368 | tf_op jit(solution)/shard_map/ppermute | solution.py:29
  90.3 1.7 %shard_map.76 = (f32[8,256,128]{2,1,0:T(8,128)S(1)}, f32[8,256,128]{2,1,0:T(8,128)S(1)}) custom-call(f32[264,256]{1,0:T(8,128)S(1)} %get-tuple-element.24.refs_0_, f32[264,256]{1,0:T(8,128)S(1)} %collective-permute-done.2.refs_1_, f32[264,256]{1,0:T(8,128)S(1)} %collective-permute-done.3.refs_2_, f32[264,256]{1,0:T(8,128)S(1)} %collective-permute-done.4.refs_3_, ...), custom_call_target="tpu_custom_call" | custom-call | tf_op jit(solution)/shard_map/pallas_call | solution.py:288
  92.0 73.7 %shard_map.77 = f32[2,8,4,128,128]{4,3,2,1,0:T(8,128)S(1)} custom-call(f32[2,8,128,128]{3,2,1,0:T(8,128)S(1)} %bitcast.46, f32[8,256,128]{2,1,0:T(8,128)S(1)} %get-tuple-element.11.own_ref, f32[8,256,128]{2,1,0:T(8,128)S(1)} %get-tuple-element.12.spill_ref), custom_call_target="tpu_custom_call" | custom-call | tf_op jit(solution)/shard_map/pallas_call | solution.py:442
  165.8 2.0 %copy.10 = f32[16,2,2,128,128]{4,3,2,1,0:T(8,128)} copy(f32[16,2,2,128,128]{4,3,2,1,0:T(8,128)S(1)} %bitcast.41) | data formatting | bytes 8388608
  (25 shorter events, 2.0 us)
Async XLA Ops:
  0.0 5.0 %collective-permute-start = (s32[2]{0:T(128)}, s32[2]{0:T(128)S(1)}, u32[]{:S(2)}, u32[]{:S(2)}) collective-permute-start(s32[2]{0:T(128)} %bitcast.47), channel_id=1, source_target_pairs={{0,4},{4,8},{8,12},{12,16},{16,20},{20,24},{24,28},{1,5},{5,9},{9,... | collective-permute-start | bytes 32 | tf_op jit(solution)/shard_map/ppermute | solution.py:24
  5.0 2.2 %copy-start = (f32[16,2,2,128,128]{4,3,2,1,0:T(8,128)S(1)}, f32[16,2,2,128,128]{4,3,2,1,0:T(8,128)}, u32[]{:S(2)}) copy-start(f32[16,2,2,128,128]{4,3,2,1,0:T(8,128)} %param.7) | copy-start | bytes 12582916
  9.1 3.1 %copy-start.4 = (s32[1,1,2]{2,1,0:T(1,128)S(1)}, s32[1,1,2]{2,1,0:T(1,128)}, u32[]{:S(2)}) copy-start(s32[1,1,2]{2,1,0:T(1,128)} %param.12) | copy-start | bytes 28
  9.1 5.2 %copy-start.3 = (f32[256,256]{1,0:T(8,128)S(1)}, f32[256,256]{1,0:T(8,128)}, u32[]{:S(2)}) copy-start(f32[256,256]{1,0:T(8,128)} %param.9) | copy-start | bytes 786436
  10.3 14.5 %collective-permute-start.1 = (f32[4,256,256]{2,1,0:T(8,128)}, f32[4,256,256]{2,1,0:T(8,128)S(1)}, u32[]{:S(2)}, u32[]{:S(2)}) collective-permute-start(f32[4,256,256]{2,1,0:T(8,128)} %get-tuple-element.15), channel_id=1, source_target_pairs={{4,0},{8,4},{12,8},{16,12},{20,16},{24,20},{28,24},{5,1},{9,5},{13... | collective-permute-start | bytes 3145736 | tf_op jit(solution)/shard_map/ppermute | solution.py:24
  15.3 13.3 %copy-start.2 = (f32[1,1,2,256,256]{4,3,2,1,0:T(8,128)S(1)}, f32[1,1,2,256,256]{4,3,2,1,0:T(8,128)}, u32[]{:S(2)}) copy-start(f32[1,1,2,256,256]{4,3,2,1,0:T(8,128)} %param.10) | copy-start | bytes 1572868
  15.4 13.3 %copy-start.1 = (f32[4,2,256,256]{3,2,1,0:T(8,128)S(1)}, f32[4,2,256,256]{3,2,1,0:T(8,128)}, u32[]{:S(2)}) copy-start(f32[4,2,256,256]{3,2,1,0:T(8,128)} %probe_ref.3) | copy-start | bytes 6291460
  24.8 19.3 %collective-permute-start.5 = (f32[4,256,256]{2,1,0:T(8,128)S(1)}, f32[4,256,256]{2,1,0:T(8,128)S(1)}, u32[]{:S(2)}, u32[]{:S(2)}) collective-permute-start(f32[4,256,256]{2,1,0:T(8,128)S(1)} %get-tuple-element.10), channel_id=1, source_target_pairs={{4,0},{8,4},{12,8},{16,12},{20,16},{24,20},{28,24},{5,1},{9,5},{13... | collective-permute-start | bytes 3145736 | tf_op jit(solution)/shard_map/ppermute | solution.py:24
  39.5 20.1 %collective-permute-start.4 = (f32[264,256]{1,0:T(8,128)S(1)}, f32[264,256]{1,0:T(8,128)S(1)}, u32[]{:S(2)}, u32[]{:S(2)}) collective-permute-start(f32[264,256]{1,0:T(8,128)S(1)} %get-tuple-element.21), channel_id=1, source_target_pairs={{0,3},{1,0},{2,1},{3,2},{4,7},{5,4},{6,5},{7,6},{8,11},{9,8},{10,9... | collective-permute-start | bytes 811016 | tf_op jit(solution)/shard_map/ppermute | solution.py:29
  43.1 24.2 %collective-permute-start.3 = (f32[264,256]{1,0:T(8,128)S(1)}, f32[264,256]{1,0:T(8,128)S(1)}, u32[]{:S(2)}, u32[]{:S(2)}) collective-permute-start(f32[264,256]{1,0:T(8,128)S(1)} %get-tuple-element.22), channel_id=1, source_target_pairs={{0,2},{1,3},{2,0},{3,1},{4,6},{5,7},{6,4},{7,5},{8,10},{9,11},{10,... | collective-permute-start | bytes 811016 | tf_op jit(solution)/shard_map/ppermute | solution.py:29
  43.1 24.2 %collective-permute-start.2 = (f32[264,256]{1,0:T(8,128)S(1)}, f32[264,256]{1,0:T(8,128)S(1)}, u32[]{:S(2)}, u32[]{:S(2)}) collective-permute-start(f32[264,256]{1,0:T(8,128)S(1)} %get-tuple-element.23), channel_id=1, source_target_pairs={{0,1},{1,2},{2,3},{3,0},{4,5},{5,6},{6,7},{7,4},{8,9},{9,10},{10,1... | collective-permute-start | bytes 811016 | tf_op jit(solution)/shard_map/ppermute | solution.py:29
  55.6 17.2 %collective-permute-start.8 = (f32[264,256]{1,0:T(8,128)}, f32[264,256]{1,0:T(8,128)S(1)}, u32[]{:S(2)}, u32[]{:S(2)}) collective-permute-start(f32[264,256]{1,0:T(8,128)} %get-tuple-element.17), channel_id=1, source_target_pairs={{0,3},{1,0},{2,1},{3,2},{4,7},{5,4},{6,5},{7,6},{8,11},{9,8},{10,9... | collective-permute-start | bytes 811016 | tf_op jit(solution)/shard_map/ppermute | solution.py:29
  58.4 31.9 %collective-permute-start.7 = (f32[264,256]{1,0:T(8,128)S(1)}, f32[264,256]{1,0:T(8,128)S(1)}, u32[]{:S(2)}, u32[]{:S(2)}) collective-permute-start(f32[264,256]{1,0:T(8,128)S(1)} %get-tuple-element.18), channel_id=1, source_target_pairs={{0,2},{1,3},{2,0},{3,1},{4,6},{5,7},{6,4},{7,5},{8,10},{9,11},{10,... | collective-permute-start | bytes 811016 | tf_op jit(solution)/shard_map/ppermute | solution.py:29
  59.6 30.7 %collective-permute-start.6 = (f32[264,256]{1,0:T(8,128)S(1)}, f32[264,256]{1,0:T(8,128)S(1)}, u32[]{:S(2)}, u32[]{:S(2)}) collective-permute-start(f32[264,256]{1,0:T(8,128)S(1)} %get-tuple-element.19), channel_id=1, source_target_pairs={{0,1},{1,2},{2,3},{3,0},{4,5},{5,6},{6,7},{7,4},{8,9},{9,10},{10,1... | collective-permute-start | bytes 811016 | tf_op jit(solution)/shard_map/ppermute | solution.py:29
